TPU v7x, 256 devices: a whole 4x4x8 slice. The times are simulated.
256 devices in a mesh: seq: 32 (over x, y, core), tensor: 8 (over z).
Axes of the slice: x: 4, y: 4, z: 8, core: 2. Of those that a mesh axis runs over, the one named last changes fastest.
Arguments:
- x_rows: bfloat16 [32768, 2304], P(('seq', 'tensor')), may hold values from -6 to 6
- w_qkv: bfloat16 [2304, 3, 4096], P('seq', None, 'tensor'), may hold values from -0.125 to 0.125
- w_beta: bfloat16 [2304, 32], P('seq', 'tensor'), may hold values from -1 to 1
- conv_weight: float32 [4, 3, 4096], P(None, None, 'tensor'), may hold values from -3 to 3
- log_decay: float32 [32768, 4096], P('seq', 'tensor'), may hold values from -1 to 0, as said below
- norm_gain: float32 [128], replicated, may hold values from 0.25 to 1.75
- w_out: bfloat16 [4096, 2304], P('tensor', 'seq'), may hold values from -0.09375 to 0.09375
Outputs:
- layer_out: bfloat16 [32768, 2304], P(('seq', 'tensor'))
Inputs may be any that keep to these rules, and one draw needn't show every extreme that they name: `log_decay`: natural logarithm of a decay factor, negative.
All inputs are finite; a program needn't handle non-finite values.
Results may differ from a plain program's by a relative error of at most 0.02.
Values may be sent and summed in bfloat16 or wider, within the bound.
A program may use at most 128 MiB of HBM per device.

v0:
```python
import jax
import jax.numpy as jnp
from jax import lax
from jax.sharding import PartitionSpec as P

BLOCK = 64


precise = lax.Precision.HIGHEST


def from_behind(array, axis, by):
    size = lax.axis_size(axis)
    pairs = [(i, i + by) for i in range(size) if 0 <= i + by < size]
    return lax.ppermute(array, axis, pairs)


def unit_rows(matrix):
    return matrix / jnp.sqrt(jnp.sum(matrix * matrix, axis=-1, keepdims=True) + 1e-06)


def chain_product(left, right):
    return jnp.einsum("...ij,...jk->...ik", left, right, precision=precise)


def block_terms(query, prng_input_vectors, values, strength, decay_logs):
    span = query.shape[-2]
    row_ids = lax.broadcasted_iota(jnp.int32, (span, span), 0)
    col_ids = lax.broadcasted_iota(jnp.int32, (span, span), 1)
    lower_incl = (row_ids >= col_ids).astype(jnp.float32)
    strict_lower = (row_ids > col_ids).astype(jnp.float32)
    cumul = jnp.einsum("rc,...cd->...rd", lower_incl, decay_logs, precision=precise)
    final = cumul[..., -1:, :]
    query_dec = query * jnp.exp(cumul)
    key_dec = prng_input_vectors * jnp.exp(cumul)
    key_inv = prng_input_vectors * jnp.exp(-cumul)
    key_end = prng_input_vectors * jnp.exp(final - cumul)
    mixing = (
        strength[..., :, None]
        * jnp.einsum("...rd,...id->...ri", key_dec, key_inv, precision=precise)
        * strict_lower
    )
    scores = jnp.einsum("...rd,...id->...ri", query_dec, key_inv, precision=precise) * lower_incl
    unit = jnp.eye(span, dtype=jnp.float32)
    inverse = unit - mixing
    powered = mixing
    for doubling in range(span.bit_length() - 2):
        powered = chain_product(powered, powered)
        inverse = chain_product(inverse, unit + powered)
    weighted_keys = chain_product(inverse, strength[..., :, None] * key_dec)
    weighted_vals = chain_product(inverse, strength[..., :, None] * values)
    reader = query_dec - chain_product(scores, weighted_keys)
    local_out = chain_product(scores, weighted_vals)
    head_size = query.shape[-1]
    diagonal = jnp.exp(final)[..., 0, :, None] * jnp.eye(head_size, dtype=jnp.float32)
    transit = diagonal - jnp.einsum("...id,...ie->...de", key_end, weighted_keys, precision=precise)
    inject = jnp.einsum("...id,...ie->...de", key_end, weighted_vals, precision=precise)
    return (reader, local_out, transit, inject)


def per_device(x_rows, w_qkv, w_beta, conv_weight, log_decay, norm_gain, w_out):
    tokens_full = lax.all_gather(x_rows, "tensor", axis=0, tiled=True)
    length = tokens_full.shape[0]
    channels = w_qkv.shape[2]
    heads_here = w_beta.shape[1]
    head_size = channels // heads_here
    taps = conv_weight.shape[0]
    pieces = (
        lax.all_gather(w_qkv, "seq", axis=0, tiled=True),
        lax.all_gather(w_beta, "seq", axis=0, tiled=True),
    )
    count = pieces[0].shape[0]
    flat_piece = pieces[0].reshape(count, 3 * channels)
    first = jnp.dot(tokens_full, flat_piece, preferred_element_type=jnp.float32)
    second = jnp.dot(tokens_full, pieces[1], preferred_element_type=jnp.float32)
    projected = first
    projected = projected.astype(jnp.bfloat16).reshape(length, 3, channels)
    earlier_rim = from_behind(projected[length - (taps - 1) :], "seq", 1)
    padded = jnp.concatenate([earlier_rim, projected], axis=0)
    summed = jnp.zeros((length, 3, channels), jnp.float32)
    for offset in range(taps):
        summed = summed + conv_weight[offset] * padded[offset : offset + length].astype(jnp.float32)
    convolved = jax.nn.silu(summed)
    query = unit_rows(convolved[:, 0].reshape(length, heads_here, head_size))
    prng_input_vectors = unit_rows(convolved[:, 1].reshape(length, heads_here, head_size))
    values = convolved[:, 2].reshape(length, heads_here, head_size)
    strength = jax.nn.sigmoid(second)
    blocks = length // BLOCK

    def to_blocks(matrix):
        return matrix.reshape(blocks, BLOCK, heads_here, head_size).transpose(0, 2, 1, 3)

    reader, local_out, transit, inject = block_terms(
        to_blocks(query),
        to_blocks(prng_input_vectors),
        to_blocks(values),
        strength.reshape(blocks, BLOCK, heads_here).transpose(0, 2, 1),
        to_blocks(log_decay.reshape(length, heads_here, head_size)),
    )
    identity = jnp.broadcast_to(
        jnp.eye(head_size, dtype=jnp.float32), (heads_here, head_size, head_size)
    )
    zero_state = jnp.zeros((heads_here, head_size, head_size), jnp.float32)

    def walk_maps(carry, element):
        state_now, through = carry
        step_map, step_add = element
        return (
            (chain_product(step_map, state_now) + step_add, chain_product(step_map, through)),
            None,
        )

    (end_state, composite), unused = lax.scan(walk_maps, (zero_state, identity), (transit, inject))

    def relay(counter, carry):
        leaving, arriving = carry
        arriving = from_behind(leaving.astype(jnp.bfloat16), "seq", 1).astype(leaving.dtype)
        return (chain_product(composite, arriving) + end_state, arriving)

    entering = lax.fori_loop(0, lax.axis_size("seq") - 1, relay, (end_state, zero_state))[1]

    def replay(state_now, element):
        read_now, own_out, step_map, step_add = element
        emitted = chain_product(read_now, state_now) + own_out
        return (chain_product(step_map, state_now) + step_add, emitted)

    attended_blocks = lax.scan(replay, entering, (reader, local_out, transit, inject))[1]
    attended = attended_blocks.transpose(0, 2, 1, 3).reshape(length, heads_here, head_size)
    scale_rows = lax.rsqrt(jnp.mean(attended * attended, axis=-1, keepdims=True) + 1e-05)
    normed = (attended * scale_rows * norm_gain).astype(jnp.bfloat16).reshape(length, channels)
    out_weights = lax.all_gather(w_out, "seq", axis=1, tiled=True)
    return lax.psum_scatter(
        jnp.dot(normed, out_weights, preferred_element_type=jnp.float32).astype(jnp.bfloat16),
        "tensor",
        scatter_dimension=0,
        tiled=True,
    )


def solution(mesh):
    in_specs = (
        P(("seq", "tensor"), None),
        P("seq", None, "tensor"),
        P("seq", "tensor"),
        P(None, None, "tensor"),
        P("seq", "tensor"),
        P(),
        P("tensor", "seq"),
    )
    out_specs = P(("seq", "tensor"), None)
    return jax.shard_map(
        per_device, mesh=mesh, in_specs=in_specs, out_specs=out_specs, check_vma=False
    )
```

profile of v0, /device:TPU:1, one launch (start us, length us, event | category | flops | bytes accessed | tf_op | source)
XLA Modules:
  0.0 757.5 jit_solution(3981613765902350872)
XLA Ops:
  9.8 3.0 reshape_reshape.3
  12.8 2.8 fusion.48
  15.6 25.8 %all-gather = bf16[32,72,4]{1,2,0:T(4,128)(2,1)S(1)} all-gather(bf16[1,72,4]{1,2,0:T(4,128)(2,1)S(1)} %bitcast.174), channel_id=1, replica_groups=mesh['seq'=32,'tensor'=8] {'seq'}, dimensions={0}, use_global_device_ids=true | all-gather | bytes 19008 | tf_op jit(solution)/shard_map/all_gather | solution.py:70
  41.7 28.0 %all-gather.7.cloned.1.call-done = bf16[2304,3,512]{2,0,1:T(8,128)(2,1)} async-done(((bf16[72,3,512]{2,0,1:T(8,128)(2,1)}), bf16[2304,3,512]{2,0,1:T(8,128)(2,1)}) %all-gather.7.cloned.1.call-update) | async-done | bytes 7077904 | tf_op jit(solution)/shard_map/all_gather | solution.py:69
  69.7 9.8 %copy.58 = bf16[2304,3,512]{0,2,1:T(8,128)(2,1)} copy(bf16[2304,3,512]{2,0,1:T(8,128)(2,1)} %all-gather.7.cloned.1.call-done) | data formatting | bytes 14155776 | tf_op jit(solution)/shard_map/all_gather | solution.py:69
  79.4 50.5 %all-gather.5.cloned.1.call-done = bf16[1024,2304]{1,0:T(8,128)(2,1)} async-done(((bf16[128,2304]{1,0:T(8,128)(2,1)}), bf16[1024,2304]{1,0:T(8,128)(2,1)}) %all-gather.5.cloned.1.call-update) | async-done | bytes 4718608 | tf_op jit(solution)/shard_map/all_gather | solution.py:62
  129.9 11.1 %convolution_convert_fusion.1 = bf16[1024,1536]{1,0:T(8,128)(2,1)S(1)} fusion(bf16[1024,2304]{1,0:T(8,128)(2,1)} %all-gather.5.cloned.1.call-done, bf16[2304,1536]{0,1:T(8,128)(2,1)} %bitcast.162), kind=kOutput, calls=%fused_computation.28 | convolution fusion | flops 7249330176 | bytes 14942208 | tf_op jit(solution)/shard_map/dot_general | solution.py:74
  143.0 3.9 collective-permute-start.1
  146.9 3.7 fusion.53
  150.7 4.7 copy.60
  155.4 12.3 %divide_multiply_fusion = f32[1024,3,512]{0,2,1:T(8,128)S(1)} fusion(bf16[1024,3,512]{0,2,1:T(8,128)(2,1)} %bitcast.158, bf16[3,3,512]{0,2,1:T(8,128)(2,1)S(1)} %collective-permute-done.1, f32[3,512]{1,0:T(4,128)S(1)} %get-tuple-element.163, f32[3,512]{1,0:T(4,128)S(1)} %get-tuple-element.164, f32[3,512]{1,0:T(4,128)S(1)} %get-tuple-element.165, ...), kind=kLoop, calls=%fused_computation.23 | loop fusion | flops 37748736 | bytes 9470976 | tf_op jit(solution)/shard_map/jit(silu)/mul | solution.py:83
  167.7 4.5 slice_multiply_fusion
  172.2 4.5 reshape.106
  176.7 3.9 copy.63
  182.5 4.5 reshape.108
  187.0 3.8 copy.70
  192.7 7.0 fusion.69
  216.8 3.6 fusion.85
  220.4 3.6 fusion.31
  224.0 4.5 reshape.107
  228.5 4.1 copy.67
  232.6 4.7 fusion.29
  237.3 3.6 fusion.27
  243.2 4.7 fusion.70
  248.0 3.7 fusion.40
  251.7 4.4 fusion.45
  256.1 9.2 %fusion.71 = f32[16,4,128,128]{3,2,1,0:T(8,128)} fusion(f32[16,4,64,128]{3,2,1,0:T(8,128)S(1)} %fusion.23, f32[16,4,64,128]{3,2,1,0:T(8,128)S(1)} %fusion.48, f32[16,4,128]{2,1,0:T(4,128)S(1)} %bitcast.171, f32[16,64,4,128]{3,1,2,0:T(8,128)S(1)} %copy-done.2, f32[16,64,4]{1,2,0:T(4,128)S(1)} %copy.62), kind=kOutput, calls=%fused_computation.89 | convolution fusion | flops 806879232 | bytes 10534912 | tf_op jit(solution)/shard_map/...id,...ie->...de/dot_general | solution.py:57
  265.3 9.6 %multiply_subtract_fusion = f32[16,4,128,128]{3,2,1,0:T(8,128)} fusion(f32[16,4,64,128]{3,2,1,0:T(8,128)S(1)} %fusion.27, f32[128,128]{1,0:T(8,128)S(1)} %fusion.72, f32[16,4,128]{2,1,0:T(4,128)S(1)} %bitcast.173, f32[16,4,64,128]{3,2,1,0:T(8,128)S(1)} %fusion.48, f32[16,4,128]{2,1,0:T(4,128)S(1)} %bitcast.172, f32[16,64,4,128]{3,1,2,0:T(8,128)S(1)} %copy-done.2, ...), kind=kOutput, calls=%fused_computation.27 | convolution fusion | flops 808976384 | bytes 10633216 | tf_op jit(solution)/shard_map/...id,...ie->...de/dot_general | solution.py:56
  275.0 45.9 %while.39 = (s32[]{:T(128)}, f32[4,128,128]{2,1,0:T(8,128)S(1)}, f32[4,128,128]{2,1,0:T(8,128)S(1)}, f32[16,4,128,128]{3,2,1,0:T(8,128)}, f32[16,4,128,128]{3,2,1,0:T(8,128)}, /*index=5*/s32[]{:T(128)}, s32[]{:T(128)}) while((s32[]{:T(128)}, f32[4,128,128]{2,1,0:T(8,128)S(1)}, f32[4,128,128]{2,1,0:T(8,128)S(1)}, ...), condition=%wide.region_2.3_spmd.clone, body=%wide.region_1.2_spmd.clone.sunk | while | flops 201457664 | bytes 2885207 | solution.py:113
  320.9 262.0 %while.37 = (s32[]{:T(128)}, bf16[4,128,128]{2,1,0:T(8,128)(2,1)S(1)}, f32[4,128,128]{2,1,0:T(8,128)}, f32[4,128,128]{2,1,0:T(8,128)S(1)}, f32[4,128,128]{2,1,0:T(8,128)S(1)}, /*index=5*/s32[]{:T(128)}) while((s32[]{:T(128)}, bf16[4,128,128]{2,1,0:T(8,128)(2,1)S(1)}, f32[4,128,128]{2,1,0:T(8,128)}, f32[4,128,128]{2,1,0:T(8,128)S(1)}, ...), condition=%wide.region_4.5_spmd, body=%wide.region_3.4_spmd.sunk | while | flops 100859904 | bytes 1704045 | solution.py:120
  325.8 4.4 collective-permute-start
  333.1 4.4 collective-permute-start
  340.4 4.4 collective-permute-start
  347.7 4.4 collective-permute-start
  355.0 4.4 collective-permute-start
  362.2 4.4 collective-permute-start
  369.5 4.4 collective-permute-start
  376.8 4.4 collective-permute-start
  384.1 4.4 collective-permute-start
  391.4 4.4 collective-permute-start
  398.7 4.4 collective-permute-start
  406.0 5.0 collective-permute-start
  413.9 6.5 collective-permute-start
  423.2 6.5 collective-permute-start
  432.6 6.5 collective-permute-start
  442.0 6.5 collective-permute-start
  451.4 6.5 collective-permute-start
  460.8 6.5 collective-permute-start
  470.2 6.5 collective-permute-start
  479.6 6.5 collective-permute-start
  489.0 6.5 collective-permute-start
  498.4 6.5 collective-permute-start
  507.8 6.5 collective-permute-start
  517.2 6.5 collective-permute-start
  526.6 6.5 collective-permute-start
  536.0 6.5 collective-permute-start
  545.4 6.5 collective-permute-start
  554.8 6.5 collective-permute-start
  564.2 6.5 collective-permute-start
  573.6 6.5 collective-permute-start
  583.0 70.6 %while.38 = (s32[]{:T(128)}, f32[4,128,128]{2,1,0:T(8,128)}, f32[16,4,64,128]{3,2,1,0:T(8,128)S(1)}, f32[16,4,128,128]{3,2,1,0:T(8,128)}, f32[16,4,128,128]{3,2,...) while((s32[]{:T(128)}, f32[4,128,128]{2,1,0:T(8,128)}, ...), condition=%wide.region_7.8_spmd, body=%wide.region_6.7_spmd.sunk | while | flops 151093248 | bytes 2230357 | solution.py:127
  654.5 2.8 copy.71
  658.9 6.0 convolution_convert_fusion
  664.9 85.6 %reduce-scatter.2.cloned.1.call-done = bf16[128,2304]{1,0:T(8,128)(2,1)} async-done(((bf16[1024,2304]{1,0:T(8,128)(2,1)}), bf16[128,2304]{1,0:T(8,128)(2,1)}) %reduce-scatter.2.cloned.1.call-update) | async-done | bytes 589840 | tf_op jit(solution)/shard_map/reduce_scatter | solution.py:132
  (274 shorter events, 238.4 us)
Async XLA Ops:
  6.5 35.1 %copy-start = (f32[128]{0:T(128)S(1)}, f32[128]{0:T(128)}, u32[]{:S(2)}) copy-start(f32[128]{0:T(128)} %param.18) | copy-start | bytes 1540
  6.5 63.1 %all-gather.7.cloned.1.call-start = ((), (), s32[]{:S(2)}) async-start(), calls=%async_computation.2 | async-start | bytes 7299072 | tf_op jit(solution)/shard_map/all_gather | solution.py:69
  7.3 122.7 %all-gather.5.cloned.1.call-start = ((), (), s32[]{:S(2)}) async-start(), calls=%async_computation.1 | async-start | bytes 5308416 | tf_op jit(solution)/shard_map/all_gather | solution.py:62
  8.0 649.3 %all-gather.9.cloned.1.call-start = ((), (), s32[]{:S(2)}) async-start(), calls=%async_computation.3 | async-start | bytes 2433024 | tf_op jit(solution)/shard_map/all_gather | solution.py:131
  8.7 741.8 %reduce-scatter.2.cloned.1.call-start = ((), (), s32[]{:S(2)}) async-start(), calls=%async_computation.4 | async-start | bytes 5308416 | tf_op jit(solution)/shard_map/reduce_scatter | solution.py:132
  12.8 2.9 copy-start.8
  141.1 1.6 copy-start.6
  143.0 12.4 %collective-permute-start.1 = (bf16[3,3,512]{0,2,1:T(8,128)(2,1)S(1)}, bf16[3,3,512]{0,2,1:T(8,128)(2,1)S(1)}, u32[]{:S(2)}, u32[]{:S(2)}) collective-permute-start(bf16[3,3,512]{0,2,1:T(8,128)(2,1)S(1)} %bitcast.170), channel_id=1, source_target_pairs={{0,8},{8,16},{16,24},{24,32},{32,40},{40,48},{48,56},{56,64},{64,7... | collective-permute-start | bytes 27656 | tf_op jit(solution)/shard_map/ppermute | solution.py:15
  232.6 4.7 copy-start.2
  237.3 3.6 copy-start.4
  240.9 2.3 copy-start.3
  275.0 308.0 %copy-start.5 = (f32[16,4,64,128]{3,2,1,0:T(8,128)S(1)}, f32[16,4,64,128]{3,2,1,0:T(8,128)}, u32[]{:S(2)}) copy-start(f32[16,4,64,128]{3,2,1,0:T(8,128)} %custom-call.2) | copy-start | bytes 6291460
  321.0 3.9 collective-permute-start
  325.8 6.3 collective-permute-start
  333.1 6.3 collective-permute-start
  340.4 6.3 collective-permute-start
  347.7 6.3 collective-permute-start
  355.0 6.3 collective-permute-start
  362.2 6.3 collective-permute-start
  369.5 6.3 collective-permute-start
  376.8 6.3 collective-permute-start
  384.1 6.3 collective-permute-start
  391.4 6.3 collective-permute-start
  398.7 6.3 collective-permute-start
  406.0 6.9 collective-permute-start
  413.9 8.4 %collective-permute-start = (bf16[4,128,128]{2,1,0:T(8,128)(2,1)S(1)}, bf16[4,128,128]{2,1,0:T(8,128)(2,1)S(1)}, u32[]{:S(2)}, u32[]{:S(2)}) collective-permute-start(bf16[4,128,128]{2,1,0:T(8,128)(2,1)S(1)} %get-tuple-element.298), channel_id=1, source_target_pairs={{0,8},{8,16},{16,24},{24,32},{32,40},{40,48},{48,56},{56,64},{64,7... | collective-permute-start | bytes 393224 | tf_op jit(solution)/shard_map/while/body/eval_jaxpr/ppermute | solution.py:15
  423.2 8.4 %collective-permute-start = (bf16[4,128,128]{2,1,0:T(8,128)(2,1)S(1)}, bf16[4,128,128]{2,1,0:T(8,128)(2,1)S(1)}, u32[]{:S(2)}, u32[]{:S(2)}) collective-permute-start(bf16[4,128,128]{2,1,0:T(8,128)(2,1)S(1)} %get-tuple-element.298), channel_id=1, source_target_pairs={{0,8},{8,16},{16,24},{24,32},{32,40},{40,48},{48,56},{56,64},{64,7... | collective-permute-start | bytes 393224 | tf_op jit(solution)/shard_map/while/body/eval_jaxpr/ppermute | solution.py:15
  432.6 8.4 %collective-permute-start = (bf16[4,128,128]{2,1,0:T(8,128)(2,1)S(1)}, bf16[4,128,128]{2,1,0:T(8,128)(2,1)S(1)}, u32[]{:S(2)}, u32[]{:S(2)}) collective-permute-start(bf16[4,128,128]{2,1,0:T(8,128)(2,1)S(1)} %get-tuple-element.298), channel_id=1, source_target_pairs={{0,8},{8,16},{16,24},{24,32},{32,40},{40,48},{48,56},{56,64},{64,7... | collective-permute-start | bytes 393224 | tf_op jit(solution)/shard_map/while/body/eval_jaxpr/ppermute | solution.py:15
  442.0 8.4 %collective-permute-start = (bf16[4,128,128]{2,1,0:T(8,128)(2,1)S(1)}, bf16[4,128,128]{2,1,0:T(8,128)(2,1)S(1)}, u32[]{:S(2)}, u32[]{:S(2)}) collective-permute-start(bf16[4,128,128]{2,1,0:T(8,128)(2,1)S(1)} %get-tuple-element.298), channel_id=1, source_target_pairs={{0,8},{8,16},{16,24},{24,32},{32,40},{40,48},{48,56},{56,64},{64,7... | collective-permute-start | bytes 393224 | tf_op jit(solution)/shard_map/while/body/eval_jaxpr/ppermute | solution.py:15
  451.4 8.4 %collective-permute-start = (bf16[4,128,128]{2,1,0:T(8,128)(2,1)S(1)}, bf16[4,128,128]{2,1,0:T(8,128)(2,1)S(1)}, u32[]{:S(2)}, u32[]{:S(2)}) collective-permute-start(bf16[4,128,128]{2,1,0:T(8,128)(2,1)S(1)} %get-tuple-element.298), channel_id=1, source_target_pairs={{0,8},{8,16},{16,24},{24,32},{32,40},{40,48},{48,56},{56,64},{64,7... | collective-permute-start | bytes 393224 | tf_op jit(solution)/shard_map/while/body/eval_jaxpr/ppermute | solution.py:15
  460.8 8.4 %collective-permute-start = (bf16[4,128,128]{2,1,0:T(8,128)(2,1)S(1)}, bf16[4,128,128]{2,1,0:T(8,128)(2,1)S(1)}, u32[]{:S(2)}, u32[]{:S(2)}) collective-permute-start(bf16[4,128,128]{2,1,0:T(8,128)(2,1)S(1)} %get-tuple-element.298), channel_id=1, source_target_pairs={{0,8},{8,16},{16,24},{24,32},{32,40},{40,48},{48,56},{56,64},{64,7... | collective-permute-start | bytes 393224 | tf_op jit(solution)/shard_map/while/body/eval_jaxpr/ppermute | solution.py:15
  470.2 8.4 %collective-permute-start = (bf16[4,128,128]{2,1,0:T(8,128)(2,1)S(1)}, bf16[4,128,128]{2,1,0:T(8,128)(2,1)S(1)}, u32[]{:S(2)}, u32[]{:S(2)}) collective-permute-start(bf16[4,128,128]{2,1,0:T(8,128)(2,1)S(1)} %get-tuple-element.298), channel_id=1, source_target_pairs={{0,8},{8,16},{16,24},{24,32},{32,40},{40,48},{48,56},{56,64},{64,7... | collective-permute-start | bytes 393224 | tf_op jit(solution)/shard_map/while/body/eval_jaxpr/ppermute | solution.py:15
  479.6 8.4 %collective-permute-start = (bf16[4,128,128]{2,1,0:T(8,128)(2,1)S(1)}, bf16[4,128,128]{2,1,0:T(8,128)(2,1)S(1)}, u32[]{:S(2)}, u32[]{:S(2)}) collective-permute-start(bf16[4,128,128]{2,1,0:T(8,128)(2,1)S(1)} %get-tuple-element.298), channel_id=1, source_target_pairs={{0,8},{8,16},{16,24},{24,32},{32,40},{40,48},{48,56},{56,64},{64,7... | collective-permute-start | bytes 393224 | tf_op jit(solution)/shard_map/while/body/eval_jaxpr/ppermute | solution.py:15
  489.0 8.4 %collective-permute-start = (bf16[4,128,128]{2,1,0:T(8,128)(2,1)S(1)}, bf16[4,128,128]{2,1,0:T(8,128)(2,1)S(1)}, u32[]{:S(2)}, u32[]{:S(2)}) collective-permute-start(bf16[4,128,128]{2,1,0:T(8,128)(2,1)S(1)} %get-tuple-element.298), channel_id=1, source_target_pairs={{0,8},{8,16},{16,24},{24,32},{32,40},{40,48},{48,56},{56,64},{64,7... | collective-permute-start | bytes 393224 | tf_op jit(solution)/shard_map/while/body/eval_jaxpr/ppermute | solution.py:15
  498.4 8.4 %collective-permute-start = (bf16[4,128,128]{2,1,0:T(8,128)(2,1)S(1)}, bf16[4,128,128]{2,1,0:T(8,128)(2,1)S(1)}, u32[]{:S(2)}, u32[]{:S(2)}) collective-permute-start(bf16[4,128,128]{2,1,0:T(8,128)(2,1)S(1)} %get-tuple-element.298), channel_id=1, source_target_pairs={{0,8},{8,16},{16,24},{24,32},{32,40},{40,48},{48,56},{56,64},{64,7... | collective-permute-start | bytes 393224 | tf_op jit(solution)/shard_map/while/body/eval_jaxpr/ppermute | solution.py:15
  507.8 8.4 %collective-permute-start = (bf16[4,128,128]{2,1,0:T(8,128)(2,1)S(1)}, bf16[4,128,128]{2,1,0:T(8,128)(2,1)S(1)}, u32[]{:S(2)}, u32[]{:S(2)}) collective-permute-start(bf16[4,128,128]{2,1,0:T(8,128)(2,1)S(1)} %get-tuple-element.298), channel_id=1, source_target_pairs={{0,8},{8,16},{16,24},{24,32},{32,40},{40,48},{48,56},{56,64},{64,7... | collective-permute-start | bytes 393224 | tf_op jit(solution)/shard_map/while/body/eval_jaxpr/ppermute | solution.py:15
  517.2 8.4 %collective-permute-start = (bf16[4,128,128]{2,1,0:T(8,128)(2,1)S(1)}, bf16[4,128,128]{2,1,0:T(8,128)(2,1)S(1)}, u32[]{:S(2)}, u32[]{:S(2)}) collective-permute-start(bf16[4,128,128]{2,1,0:T(8,128)(2,1)S(1)} %get-tuple-element.298), channel_id=1, source_target_pairs={{0,8},{8,16},{16,24},{24,32},{32,40},{40,48},{48,56},{56,64},{64,7... | collective-permute-start | bytes 393224 | tf_op jit(solution)/shard_map/while/body/eval_jaxpr/ppermute | solution.py:15
  526.6 8.4 %collective-permute-start = (bf16[4,128,128]{2,1,0:T(8,128)(2,1)S(1)}, bf16[4,128,128]{2,1,0:T(8,128)(2,1)S(1)}, u32[]{:S(2)}, u32[]{:S(2)}) collective-permute-start(bf16[4,128,128]{2,1,0:T(8,128)(2,1)S(1)} %get-tuple-element.298), channel_id=1, source_target_pairs={{0,8},{8,16},{16,24},{24,32},{32,40},{40,48},{48,56},{56,64},{64,7... | collective-permute-start | bytes 393224 | tf_op jit(solution)/shard_map/while/body/eval_jaxpr/ppermute | solution.py:15
  536.0 8.4 %collective-permute-start = (bf16[4,128,128]{2,1,0:T(8,128)(2,1)S(1)}, bf16[4,128,128]{2,1,0:T(8,128)(2,1)S(1)}, u32[]{:S(2)}, u32[]{:S(2)}) collective-permute-start(bf16[4,128,128]{2,1,0:T(8,128)(2,1)S(1)} %get-tuple-element.298), channel_id=1, source_target_pairs={{0,8},{8,16},{16,24},{24,32},{32,40},{40,48},{48,56},{56,64},{64,7... | collective-permute-start | bytes 393224 | tf_op jit(solution)/shard_map/while/body/eval_jaxpr/ppermute | solution.py:15
  545.4 8.4 %collective-permute-start = (bf16[4,128,128]{2,1,0:T(8,128)(2,1)S(1)}, bf16[4,128,128]{2,1,0:T(8,128)(2,1)S(1)}, u32[]{:S(2)}, u32[]{:S(2)}) collective-permute-start(bf16[4,128,128]{2,1,0:T(8,128)(2,1)S(1)} %get-tuple-element.298), channel_id=1, source_target_pairs={{0,8},{8,16},{16,24},{24,32},{32,40},{40,48},{48,56},{56,64},{64,7... | collective-permute-start | bytes 393224 | tf_op jit(solution)/shard_map/while/body/eval_jaxpr/ppermute | solution.py:15
  554.8 8.4 %collective-permute-start = (bf16[4,128,128]{2,1,0:T(8,128)(2,1)S(1)}, bf16[4,128,128]{2,1,0:T(8,128)(2,1)S(1)}, u32[]{:S(2)}, u32[]{:S(2)}) collective-permute-start(bf16[4,128,128]{2,1,0:T(8,128)(2,1)S(1)} %get-tuple-element.298), channel_id=1, source_target_pairs={{0,8},{8,16},{16,24},{24,32},{32,40},{40,48},{48,56},{56,64},{64,7... | collective-permute-start | bytes 393224 | tf_op jit(solution)/shard_map/while/body/eval_jaxpr/ppermute | solution.py:15
  564.2 8.4 %collective-permute-start = (bf16[4,128,128]{2,1,0:T(8,128)(2,1)S(1)}, bf16[4,128,128]{2,1,0:T(8,128)(2,1)S(1)}, u32[]{:S(2)}, u32[]{:S(2)}) collective-permute-start(bf16[4,128,128]{2,1,0:T(8,128)(2,1)S(1)} %get-tuple-element.298), channel_id=1, source_target_pairs={{0,8},{8,16},{16,24},{24,32},{32,40},{40,48},{48,56},{56,64},{64,7... | collective-permute-start | bytes 393224 | tf_op jit(solution)/shard_map/while/body/eval_jaxpr/ppermute | solution.py:15
  573.6 8.4 %collective-permute-start = (bf16[4,128,128]{2,1,0:T(8,128)(2,1)S(1)}, bf16[4,128,128]{2,1,0:T(8,128)(2,1)S(1)}, u32[]{:S(2)}, u32[]{:S(2)}) collective-permute-start(bf16[4,128,128]{2,1,0:T(8,128)(2,1)S(1)} %get-tuple-element.298), channel_id=1, source_target_pairs={{0,8},{8,16},{16,24},{24,32},{32,40},{40,48},{48,56},{56,64},{64,7... | collective-permute-start | bytes 393224 | tf_op jit(solution)/shard_map/while/body/eval_jaxpr/ppermute | solution.py:15
  657.3 1.6 copy-start.7
  664.9 85.6 %copy-start.1 = (f32[128]{0:T(128)S(1)}, f32[128]{0:T(128)}, u32[]{:S(2)}) copy-start(f32[128]{0:T(128)} %param.18) | copy-start | bytes 1540
Sparse Core Ops, SparseCore 0:
  9.9 59.6 all-gather.6
  71.5 58.4 all-gather.4
  132.5 48.6 all-gather.8
  665.0 85.4 reduce-scatter.1
where the time goes:
time: 765 us; the launch traced here: 757 us
  waiting for transfers between devices  226 us (30%)
  matrix products  205 us (27%)
  starting transfers between devices  175 us (23%)
  local copies, waits for them, and re-layouts  66.5 us (9%)
  other arithmetic  43.4 us (6%)
  blocking collectives  25.8 us (3%)
  between operations  14 us (2%)
    ppermute x32, starting transfers between devices, from_behind(): return lax.ppermute(array, axis, pairs)  175 us
    dot_general x109, matrix products, chain_product(): return jnp.einsum('...ij,...jk->...ik', left, right, precision=precise)  151 us
    reduce_scatter x1, waiting for transfers between devices, per_device(): lax.psum_scatter(jnp.dot(normed, out_weights, preferred_element_type=jnp....  85.6 us
    ppermute x32, waiting for transfers between devices, from_behind(): return lax.ppermute(array, axis, pairs)  59.7 us
    all_gather x1, waiting for transfers between devices, per_device(): tokens_full = lax.all_gather(x_rows, 'tensor', axis=0, tiled=True)  50.5 us
    all_gather x1, waiting for transfers between devices, per_device(): lax.all_gather(w_qkv, 'seq', axis=0, tiled=True)  28 us
    all_gather x1, blocking collectives, per_device(): lax.all_gather(w_beta, 'seq', axis=0, tiled=True)  25.8 us
    convert_element_type x31, other arithmetic, relay(): from_behind(leaving.astype(jnp.bfloat16), 'seq', 1).astype(leaving.dtype)  22.3 us
  transfers between devices with their start and end apart: 36, of which 34 were waited for; matrix products, arithmetic and copies ran while one was open for 40% of the time, Pallas kernels for 0%

commit v1 on v0

v1 whole, which is shorter than its diff:
```python
import functools
import jax
import jax.numpy as jnp
from jax import lax
from jax.experimental import pallas as pl
from jax.experimental.pallas import tpu as pltpu
from jax.sharding import PartitionSpec as P

f32, bf16 = jnp.float32, jnp.bfloat16
CH = 128
HD = 128


def mm(a, b):
    return jnp.dot(a.astype(bf16), b.astype(bf16), preferred_element_type=f32)


def mm_nt(a, b):
    return lax.dot_general(a.astype(bf16), b.astype(bf16), (((1,), (1,)), ((), ())), preferred_element_type=f32)


def mm_tn(a, b):
    return lax.dot_general(a.astype(bf16), b.astype(bf16), (((0,), (0,)), ((), ())), preferred_element_type=f32)


def chunk_terms(heads, load_proj, load_gate, strength, taps):
    row = lax.broadcasted_iota(jnp.int32, (CH, CH), 0)
    col = lax.broadcasted_iota(jnp.int32, (CH, CH), 1)
    incl, strict = row >= col, row > col
    lower = incl.astype(bf16)
    each = range(heads)
    width = heads * HD

    def conv(part, h):
        at = part * width + h * HD
        p = load_proj(at).astype(f32)
        y = taps[3:4, at:at + HD] * p[16:]
        for j in range(3):
            y = y + taps[j:j + 1, at:at + HD] * p[13 + j:13 + j + CH]
        return y * (0.5 + 0.5 * jnp.tanh(0.5 * y))

    def unit(m):
        return m * lax.rsqrt(jnp.sum(m * m, axis=-1, keepdims=True) + 1e-6)

    q = [unit(conv(0, h)) for h in each]
    k = [unit(conv(1, h)) for h in each]
    v = [conv(2, h) for h in each]
    b = [strength[:, h:h + 1] for h in each]
    g = [load_gate(h) for h in each]
    ghi = [m.astype(bf16) for m in g]
    glo = [(g[h] - ghi[h].astype(f32)).astype(bf16) for h in each]
    cum = [mm(lower, ghi[h]) + mm(lower, glo[h]) for h in each]
    mid = [m[CH // 2 - 1:CH // 2] for m in cum]
    fin = [m[CH - 1:CH] for m in cum]
    up = [jnp.exp(cum[h] - mid[h]) for h in each]
    down = [jnp.exp(mid[h] - cum[h]) for h in each]
    emid = [jnp.exp(mid[h]) for h in each]
    k_up = [k[h] * up[h] for h in each]
    q_up = [q[h] * up[h] for h in each]
    k_down = [k[h] * down[h] for h in each]
    k_end = [k_down[h] * jnp.exp(fin[h] - mid[h]) for h in each]
    both = [mm_nt(jnp.concatenate([k_up[h], q_up[h]], axis=0), k_down[h]) for h in each]
    mix = [jnp.where(strict, b[h] * both[h][:CH], 0.0).astype(bf16) for h in each]
    score = [jnp.where(incl, both[h][CH:], 0.0).astype(bf16) for h in each]
    eye = (row == col).astype(f32)
    zero = jnp.zeros((CH, CH), bf16)

    def off(n):
        return ((row // (2 * n)) == (col // (2 * n))) & ((row // n) % 2 == 1) & ((col // n) % 2 == 0)

    first = off(1)
    inv = [eye - jnp.where(first, mix[h], zero).astype(f32) for h in each]
    n = 2
    while n < CH:
        m = off(n)
        part = [jnp.where(m, mix[h], zero) for h in each]
        low = [inv[h].astype(bf16) for h in each]
        step = [mm(part[h], low[h]).astype(bf16) for h in each]
        inv = [inv[h] - mm(low[h], step[h]) for h in each]
        n *= 2
    q_dec = [q_up[h] * emid[h] for h in each]
    rhs = [jnp.concatenate([b[h] * (k_up[h] * emid[h]), b[h] * v[h]], axis=1).astype(bf16) for h in each]
    wu = [mm(inv[h], rhs[h]).astype(bf16) for h in each]
    sw = [mm(score[h], wu[h]) for h in each]
    kw = [mm_tn(k_end[h], wu[h]) for h in each]
    reader = [q_dec[h] - sw[h][:, :HD] for h in each]
    local = [sw[h][:, HD:] for h in each]
    erase = [kw[h][:, :HD] for h in each]
    inject = [kw[h][:, HD:] for h in each]
    final = [jnp.sum(jnp.where(row == col, jnp.exp(fin[h]), 0.0), axis=1, keepdims=True) for h in each]
    return reader, local, erase, inject, final


def k2_body(heads, proj, logit, gate, taps, rd_out, lo_out, pb_out, pb):
    c = pl.program_id(0)

    @pl.when(c == 0)
    def _():
        row = lax.broadcasted_iota(jnp.int32, (HD, 2 * HD), 0)
        col = lax.broadcasted_iota(jnp.int32, (HD, 2 * HD), 1)
        for h in range(heads):
            pb[h] = (row == col).astype(f32)

    r0 = pl.multiple_of(c * CH, CH)
    strength = 1.0 / (1.0 + jnp.exp(-logit[...]))
    reader, local, erase, inject, final = chunk_terms(
        heads,
        lambda at: proj[pl.ds(r0, CH + 16), at:at + HD],
        lambda h: gate[:, h * HD:(h + 1) * HD],
        strength, taps)
    for h in range(heads):
        now = pb[h]
        both = mm(jnp.concatenate([reader[h], erase[h]], axis=0), now)
        rd_out[:, h * HD:(h + 1) * HD] = both[:CH, :HD].astype(bf16)
        lo_out[:, h * HD:(h + 1) * HD] = (both[:CH, HD:] + local[h]).astype(lo_out.dtype)
        nxt = final[h] * now - both[CH:] + jnp.concatenate([jnp.zeros((HD, HD), f32), inject[h]], axis=1)
        pb[h] = nxt
        pb_out[h] = nxt.astype(bf16)


def k2(proj, logit, gate, taps, heads=4):
    n = gate.shape[0]
    width = heads * HD
    return pl.pallas_call(
        functools.partial(k2_body, heads),
        grid=(n // CH,),
        in_specs=[
            pl.BlockSpec(proj.shape, lambda c: (0, 0)),
            pl.BlockSpec((CH, 128), lambda c: (c, 0)),
            pl.BlockSpec((CH, width), lambda c: (c, 0)),
            pl.BlockSpec(taps.shape, lambda c: (0, 0)),
        ],
        out_specs=[
            pl.BlockSpec((CH, width), lambda c: (c, 0)),
            pl.BlockSpec((CH, width), lambda c: (c, 0)),
            pl.BlockSpec((heads, HD, 2 * HD), lambda c: (0, 0, 0)),
        ],
        out_shape=[
            jax.ShapeDtypeStruct((n, width), bf16),
            jax.ShapeDtypeStruct((n, width), bf16),
            jax.ShapeDtypeStruct((heads, HD, 2 * HD), bf16),
        ],
        scratch_shapes=[pltpu.VMEM((heads, HD, 2 * HD), f32)],
        compiler_params=pltpu.CompilerParams(vmem_limit_bytes=48 << 20),
    )(proj, logit, gate, taps)


MESH = pl.DeviceIdType.MESH
XN, YN = 4, 4
SEQ, TEN = 32, 8
PIECE = 72
PAIR = 2 * PIECE
COLS = 2304
HALF = COLS // 2
BETA_AT = 1536
OUT_AT = 1792


def place():
    s, z = lax.axis_index("seq"), lax.axis_index("tensor")
    core, chip = s % 2, s // 2
    return s, z, core, chip // YN, chip % YN


def remote(src, dst, ssem, rsem, to):
    copy = pltpu.make_async_remote_copy(src_ref=src, dst_ref=dst, send_sem=ssem, recv_sem=rsem, device_id=to, device_id_type=MESH)
    return copy


def greet(peers):
    barrier = pltpu.get_barrier_semaphore()
    for peer in peers:
        pl.semaphore_signal(barrier, inc=1, device_id=peer, device_id_type=MESH)
    pl.semaphore_wait(barrier, len(peers))


def gather_body(x, w, proj, logit, wo, xg, wf, sib, blk, rim, xs, xr, ws, wr, ss, sr, ps, pr, ls):
    s, z, core, cx, cy = place()
    a = jnp.where(core == 0, cx, cy)
    b = jnp.where(core == 0, cy, cx)

    def chip_of(da, db):
        ra, rb = (a + da) % 4, (b + db) % 4
        return jnp.where(core == 0, ra * YN + rb, rb * YN + ra)

    def dev_of(da, db):
        return (chip_of(da, db) * 2 + core, z)

    other = (s + 1 - 2 * core, z)
    right, left = (s, (z + 1) % TEN), (s, (z + TEN - 1) % TEN)
    after, before = ((s + 1) % SEQ, z), ((s + SEQ - 1) % SEQ, z)
    greet([other, right, left, dev_of(1, 0), dev_of(3, 0), dev_of(0, 1), dev_of(0, 3), after, before])

    pair = remote(w, sib, ps.at[0], pr.at[0], other)
    pair.start()
    own = pltpu.make_async_copy(x, xg.at[z], ls.at[0])
    own.start()

    def x_copy(d, k):
        c = (z + (TEN - k + 1 if d == 0 else k - 1)) % TEN
        if k == 4:
            here = xg.at[c, pl.ds(64 * d, 64)]
        else:
            here = xg.at[c]
        return remote(x if k == 1 else here, here, xs.at[d, k - 1], xr.at[d, k - 1], right if d == 0 else left)

    def x_recv(d, k):
        c = (z + (TEN - k if d == 0 else k)) % TEN
        here = xg.at[c, pl.ds(64 * d, 64)] if k == 4 else xg.at[c]
        return remote(here, here, xs.at[d, k - 1], xr.at[d, k - 1], right if d == 0 else left)

    for d in range(2):
        x_copy(d, 1).start()

    pair.wait_recv()
    mine = w[...].astype(f32)
    theirs = sib[...].astype(f32)
    blk[0:PIECE] = jnp.where(core == 0, mine, theirs)
    blk[PIECE:PAIR] = jnp.where(core == 0, theirs, mine)
    here = pl.multiple_of(chip_of(0, 0) * PAIR, 16)
    wf[pl.ds(here, PAIR)] = blk[...].astype(bf16)

    col0 = pl.multiple_of(core * HALF, 128)

    def w_ref(da, db, cols=None):
        return wf.at[pl.ds(pl.multiple_of(chip_of(da, db) * PAIR, 16), PAIR), pl.ds(col0 if cols is None else cols, HALF)]

    sends = []

    def w_send(da, db, ta, tb):
        ra, rb = (da - ta) % 4, (db - tb) % 4
        at = len(sends)
        copy = remote(w_ref(da, db), w_ref(da, db), ws.at[at], wr.at[ra * 4 + rb], dev_of(ta, tb))
        copy.start()
        sends.append(copy)

    def w_wait(da, db):
        remote(w_ref(da, db), w_ref(da, db), ws.at[0], wr.at[da * 4 + db], other).wait_recv()

    def across(da, db):
        copy = remote(w_ref(da, db), w_ref(da, db), ss.at[da * 4 + db], sr.at[da * 4 + db], other)
        copy.start()
        sends.append(copy)

    def hop_b(da):
        w_send(da, 0, 0, 1)
        w_send(da, 0, 0, 3)

    def x_forward(k):
        for d in range(2):
            x_recv(d, k).wait_recv()
            x_copy(d, k + 1).start()

    n_w = [0]
    w_send(0, 0, 1, 0)
    w_send(0, 0, 3, 0)
    hop_b(0)
    w_wait(3, 0)
    w_send(3, 0, 1, 0)
    hop_b(3)
    across(3, 0)
    w_wait(1, 0)
    hop_b(1)
    across(1, 0)
    w_wait(2, 0)
    hop_b(2)
    across(2, 0)
    w_wait(0, 3)
    w_send(0, 3, 0, 1)
    across(0, 3)
    w_wait(0, 1)
    across(0, 1)
    x_forward(1)
    for da, db in ((3, 1), (1, 3)):
        w_wait(da, db)
        w_send(da, db, 0, 3 if db == 1 else 1)
        across(da, db)
    for da, db in ((3, 3), (1, 1), (2, 1)):
        w_wait(da, db)
        if (da, db) == (2, 1):
            w_send(da, db, 0, 3)
        across(da, db)
    for da, db in ((2, 3), (0, 2), (3, 2), (1, 2), (2, 2)):
        w_wait(da, db)
        across(da, db)
    x_forward(2)
    colx = pl.multiple_of((1 - core) * HALF, 128)
    for i in range(1, 16):
        oa, ob = i // 4, i % 4
        ra, rb = ob, oa
        ref = w_ref(ra, rb, colx)
        remote(ref, ref, ss.at[i], sr.at[i], other).wait_recv()
    own.wait()
    keep = pltpu.make_async_copy(wf.at[:, pl.ds(OUT_AT, COLS - OUT_AT)], wo, ls.at[1])
    keep.start()

    rim_copy = remote(proj.at[pl.ds(TEN * CH, 16)], rim, ps.at[1], pr.at[1], after)

    def project(c):
        r = pl.multiple_of(16 + c * CH, 16)

        def tile(n, carry):
            at = pl.multiple_of(n * 256, 256)
            acc = jnp.dot(xg[c], wf[:, pl.ds(at, 256)], preferred_element_type=f32)
            proj[pl.ds(r, CH), pl.ds(at, 256)] = acc.astype(bf16)
            return carry

        lax.fori_loop(0, BETA_AT // 256, tile, 0)
        logit[pl.ds(pl.multiple_of(c * CH, CH), CH)] = jnp.dot(xg[c], wf[:, BETA_AT:BETA_AT + 128], preferred_element_type=f32)

        @pl.when((c == TEN - 1) & (s < SEQ - 1))
        def _():
            rim_copy.start()

    def around(k):
        def one(i, carry):
            project((z + jnp.where(i == 0, TEN - k, k)) % TEN)
            return carry
        lax.fori_loop(0, 2, one, 0)

    project(z)
    around(1)
    around(2)
    x_forward(3)
    around(3)
    for d in range(2):
        x_recv(d, 4).wait_recv()
    project((z + 4) % TEN)

    @pl.when(s > 0)
    def _():
        rim_copy.wait_recv()
        proj[0:16] = rim[...]

    @pl.when(s == 0)
    def _():
        proj[0:16] = jnp.zeros((16, BETA_AT), bf16)

    @pl.when(s < SEQ - 1)
    def _():
        rim_copy.wait_send()

    keep.wait()
    pair.wait_send()
    for copy in sends:
        copy.wait_send()
    for d in range(2):
        for k in range(1, 5):
            x_copy(d, k).wait_send()


def gather_project(x, w):
    return pl.pallas_call(
        gather_body,
        in_specs=[pl.BlockSpec(memory_space=pltpu.VMEM)] * 2,
        out_specs=[pl.BlockSpec(memory_space=pltpu.VMEM), pl.BlockSpec(memory_space=pltpu.VMEM), pl.BlockSpec(memory_space=pl.ANY)],
        out_shape=[
            jax.ShapeDtypeStruct((TEN * CH + 16, BETA_AT), bf16),
            jax.ShapeDtypeStruct((TEN * CH, 128), f32),
            jax.ShapeDtypeStruct((COLS, COLS - OUT_AT), bf16),
        ],
        scratch_shapes=[
            pltpu.VMEM((TEN, CH, COLS), bf16),
            pltpu.VMEM((COLS, COLS), bf16),
            pltpu.VMEM((PIECE, COLS), bf16),
            pltpu.VMEM((PAIR, COLS), f32),
            pltpu.VMEM((16, BETA_AT), bf16),
            pltpu.SemaphoreType.DMA((2, 4)),
            pltpu.SemaphoreType.DMA((2, 4)),
            pltpu.SemaphoreType.DMA((32,)),
            pltpu.SemaphoreType.DMA((16,)),
            pltpu.SemaphoreType.DMA((16,)),
            pltpu.SemaphoreType.DMA((16,)),
            pltpu.SemaphoreType.DMA((2,)),
            pltpu.SemaphoreType.DMA((2,)),
            pltpu.SemaphoreType.DMA((2,)),
        ],
        compiler_params=pltpu.CompilerParams(collective_id=0, has_side_effects=True, vmem_limit_bytes=56 << 20),
    )(x, w)


def finish_body(rd, lo, pb, gain, wo, out, sibpb, gy, pre, gx, ss, sb, sin, nrm, part, rsend, rrecv,
                csem, ysem, xsem, tsem, rssem, rrsem):
    s, z, core, cx, cy = place()
    other = (s + 1 - 2 * core, z)
    right, left = (s, (z + 1) % TEN), (s, (z + TEN - 1) % TEN)

    def y_dev(k):
        return ((cx * YN + (cy + k) % YN) * 2 + core, z)

    def x_dev(k):
        return ((((cx + k) % XN) * YN + cy) * 2 + core, z)

    greet([other, right, left] + [y_dev(k) for k in (1, 2, 3)] + [x_dev(k) for k in (1, 2, 3)])
    mine0, their0 = 2 * core, 2 - 2 * core
    first = remote(pb.at[pl.ds(their0, 2)], sibpb, csem.at[0], csem.at[1], other)
    first.start()

    def chain(later, earlier):
        p = mm(later[:, :HD], earlier)
        return p + jnp.concatenate([jnp.zeros((HD, HD), f32), later[:, HD:].astype(f32)], axis=1)

    first.wait_recv()
    heads = range(2)
    lead = []
    for i in heads:
        own, got = pb[mine0 + i], sibpb[i]
        head, tail = jnp.where(core == 0, own, got), jnp.where(core == 0, got, own)
        lead.append(head)
        gy[cy, i] = chain(tail, head).astype(bf16)
    y_copies = [remote(gy.at[cy], gy.at[cy], ysem.at[0, k], ysem.at[1, k], y_dev(k)) for k in (1, 2, 3)]
    for copy in y_copies:
        copy.start()
    for k in (1, 2, 3):
        slot = gy.at[(cy + YN - k) % YN]
        remote(slot, slot, ysem.at[0, k], ysem.at[1, k], y_dev(k)).wait_recv()
    eye = (lax.broadcasted_iota(jnp.int32, (HD, 2 * HD), 0) == lax.broadcasted_iota(jnp.int32, (HD, 2 * HD), 1)).astype(bf16)
    run = [gy[0, i] for i in heads]
    for i in heads:
        pre[0, i] = eye
        pre[1, i] = run[i]
    for k in (1, 2, 3):
        run = [chain(gy[k, i], run[i]).astype(bf16) for i in heads]
        for i in heads:
            if k < 3:
                pre[k + 1, i] = run[i]
            else:
                gx[cx, i] = run[i]
    x_copies = [remote(gx.at[cx], gx.at[cx], xsem.at[0, k], xsem.at[1, k], x_dev(k)) for k in (1, 2, 3)]
    for copy in x_copies:
        copy.start()
    for k in (1, 2, 3):
        slot = gx.at[(cx + XN - k) % XN]
        remote(slot, slot, xsem.at[0, k], xsem.at[1, k], x_dev(k)).wait_recv()
    state = [jnp.zeros((HD, HD), f32) for i in heads]
    for i in heads:
        ss[0, i] = state[i]
    for k in range(3):
        state = [mm(gx[k, i, :, :HD], state[i]) + gx[k, i, :, HD:].astype(f32) for i in heads]
        for i in heads:
            ss[k + 1, i] = state[i]
    for i in heads:
        entry = mm(pre[cy, i, :, :HD], ss[cx, i]) + pre[cy, i, :, HD:].astype(f32)
        behind = mm(lead[i][:, :HD], entry) + lead[i][:, HD:].astype(f32)
        sin[mine0 + i] = jnp.where(core == 0, entry, behind).astype(bf16)
        sb[i] = jnp.where(core == 0, behind, entry).astype(bf16)
    last = remote(sb, sin.at[pl.ds(mine0, 2)], csem.at[2], csem.at[3], other)
    last.start()
    their = sin.at[pl.ds(their0, 2)]
    remote(their, their, csem.at[2], csem.at[3], other).wait_recv()

    def attend(c):
        r = pl.ds(pl.multiple_of(c * CH, CH), CH)
        att = [mm(rd[r, h * HD:(h + 1) * HD], sin[h]) + lo[r, h * HD:(h + 1) * HD].astype(f32) for h in range(4)]
        for h in range(4):
            scale = lax.rsqrt(jnp.mean(att[h] * att[h], axis=-1, keepdims=True) + 1e-5)
            nrm[c, :, h * HD:(h + 1) * HD] = (att[h] * scale * gain[...]).astype(bf16)

    def partial(d, c):
        for n in range(0, HALF, 384):
            part[d, :, n:n + 384] = mm_nt(nrm[c], wo[d * HALF + n:d * HALF + n + 384])

    def chunk(d, t):
        return (z + (2 * TEN - 1 - t if d == 0 else 1 + t)) % TEN

    def send(d, t, u):
        rows = pl.ds(u * 64, 64)
        return remote(rsend.at[d, t, rows], rrecv.at[d, t, rows], rssem.at[d, t, u], rrsem.at[d, t, u], right if d == 0 else left)

    for d in range(2):
        c = chunk(d, 0)
        attend(c)
        partial(d, c)
        for u in range(2):
            rsend[d, 0, u * 64:u * 64 + 64] = part[d, u * 64:u * 64 + 64].astype(bf16)
            send(d, 0, u).start()

    def step(t, carry):
        for d in range(2):
            c = chunk(d, t)

            @pl.when((t < 3) | ((t == 3) & (d == 0)))
            def _():
                attend(c)

            partial(d, c)
        for u in range(2):
            for d in range(2):
                send(d, t - 1, u).wait_recv()
                total = part[d, u * 64:u * 64 + 64] + rrecv[d, t - 1, u * 64:u * 64 + 64].astype(f32)
                rsend[d, t, u * 64:u * 64 + 64] = total.astype(bf16)
                send(d, t, u).start()
        return carry

    lax.fori_loop(1, 7, step, 0)
    attend(z)
    for d in range(2):
        partial(d, z)
    for u in range(2):
        for d in range(2):
            send(d, 6, u).wait_recv()
            total = part[d, u * 64:u * 64 + 64] + rrecv[d, 6, u * 64:u * 64 + 64].astype(f32)
            out[u * 64:u * 64 + 64, d * HALF:(d + 1) * HALF] = total.astype(bf16)

    first.wait_send()
    last.wait_send()
    for copy in y_copies + x_copies:
        copy.wait_send()

    def drain(t, carry):
        for d in range(2):
            for u in range(2):
                send(d, t, u).wait_send()
        return carry

    lax.fori_loop(0, 7, drain, 0)


def finish(rd, lo, pb, gain, wo):
    return pl.pallas_call(
        finish_body,
        in_specs=[pl.BlockSpec(memory_space=pltpu.VMEM)] * 5,
        out_specs=pl.BlockSpec(memory_space=pltpu.VMEM),
        out_shape=jax.ShapeDtypeStruct((CH, COLS), bf16),
        scratch_shapes=[
            pltpu.VMEM((2, HD, 2 * HD), bf16),
            pltpu.VMEM((YN, 2, HD, 2 * HD), bf16),
            pltpu.VMEM((YN, 2, HD, 2 * HD), bf16),
            pltpu.VMEM((XN, 2, HD, 2 * HD), bf16),
            pltpu.VMEM((XN, 2, HD, HD), f32),
            pltpu.VMEM((2, HD, HD), bf16),
            pltpu.VMEM((4, HD, HD), bf16),
            pltpu.VMEM((TEN, CH, 4 * HD), bf16),
            pltpu.VMEM((2, CH, HALF), f32),
            pltpu.VMEM((2, 7, CH, HALF), bf16),
            pltpu.VMEM((2, 7, CH, HALF), bf16),
            pltpu.SemaphoreType.DMA((4,)),
            pltpu.SemaphoreType.DMA((2, 4)),
            pltpu.SemaphoreType.DMA((2, 4)),
            pltpu.SemaphoreType.DMA((2,)),
            pltpu.SemaphoreType.DMA((2, 7, 2)),
            pltpu.SemaphoreType.DMA((2, 7, 2)),
        ],
        compiler_params=pltpu.CompilerParams(collective_id=1, has_side_effects=True, vmem_limit_bytes=56 << 20),
    )(rd, lo, pb, gain, wo)


def per_device(x_rows, w_qkv, w_beta, conv_weight, log_decay, norm_gain, w_out):
    packed = jnp.concatenate(
        [w_qkv.reshape(PIECE, BETA_AT), jnp.pad(w_beta, ((0, 0), (0, OUT_AT - BETA_AT - w_beta.shape[1]))), w_out.T], axis=1)
    proj, logit, wo = gather_project(x_rows, packed)
    rd, lo, pb = k2(proj, logit, log_decay, conv_weight.reshape(4, BETA_AT))
    return finish(rd, lo, pb, norm_gain.reshape(1, HD), wo)


def solution(mesh):
    in_specs = (
        P(("seq", "tensor"), None),
        P("seq", None, "tensor"),
        P("seq", "tensor"),
        P(None, None, "tensor"),
        P("seq", "tensor"),
        P(),
        P("tensor", "seq"),
    )
    return jax.shard_map(per_device, mesh=mesh, in_specs=in_specs, out_specs=P(("seq", "tensor"), None), check_vma=False)
```

time: 765 us -> 185 us (0.24)
  waiting for transfers between devices: 226 us -> 0 us
  matrix products: 205 us -> 0 us
  starting transfers between devices: 175 us -> 0 us
  Pallas kernels: 0 us -> 174 us
  local copies, waits for them, and re-layouts: 66.5 us -> 9.71 us
  other arithmetic: 43.4 us -> 1.64 us
  blocking collectives: 25.8 us -> 0 us
  between operations: 14 us -> 0.05 us
    dot_general x117 -> x0, matrix products: 205 us -> none  [the longest x109 151 us: chain_product(): return jnp.einsum('...ij,...jk->...ik', left, right, precision=precise)]
    ppermute x32 -> x0, starting transfers between devices: 175 us -> none  [from_behind(): return lax.ppermute(array, axis, pairs)]
    pallas_call x0 -> x3, Pallas kernels: none -> 174 us  [the longest x1 74.2 us: finish(): pl.pallas_call(finish_body, in_specs=[pl.BlockSpec(memory_space=pltpu.VME...]
    reduce_scatter x1 -> x0, waiting for transfers between devices: 85.6 us -> none  [per_device(): lax.psum_scatter(jnp.dot(normed, out_weights, preferred_element_type=jnp....]
    all_gather x3 -> x0, waiting for transfers between devices: 78.5 us -> none  [the longest x1 50.5 us: per_device(): tokens_full = lax.all_gather(x_rows, 'tensor', axis=0, tiled=True)]
    ppermute x32 -> x0, waiting for transfers between devices: 59.7 us -> none  [from_behind(): return lax.ppermute(array, axis, pairs)]
    another operation x7 -> x0, local copies, waits for them, and re-layouts: 28.3 us -> none  [the longest x3 11.5 us: to_blocks(): matrix.reshape(blocks, BLOCK, heads_here, head_size).transpose(0, 2, 1, 3)]
    all_gather x1 -> x0, blocking collectives: 25.8 us -> none  [per_device(): lax.all_gather(w_beta, 'seq', axis=0, tiled=True)]
  transfers between devices with their start and end apart: 36 -> 0, of which waited for: 34 -> 0; matrix products, arithmetic and copies ran while one was open for 40% -> 0% of each run, Pallas kernels for 0% -> 0%
where the time goes in v1:
time: 185 us
  Pallas kernels  174 us (94%)
  local copies, waits for them, and re-layouts  9.71 us (5%)
    pallas_call x1, Pallas kernels, finish(): pl.pallas_call(finish_body, in_specs=[pl.BlockSpec(memory_space=pltpu.VME...  74.2 us
    pallas_call x1, Pallas kernels, gather_project(): pl.pallas_call(gather_body, in_specs=[pl.BlockSpec(memory_space=pltpu.VME...  71.8 us
    pallas_call x1, Pallas kernels, k2(): pl.pallas_call(functools.partial(k2_body, heads), grid=(n // CH,), in_spe...  27.5 us
    unnamed x14, local copies, waits for them, and re-layouts  8.76 us

profile of v1, /device:TPU:1, one launch (start us, length us, event | category | flops | bytes accessed | tf_op | source)
XLA Modules:
  0.0 184.9 jit_solution(8667739841556875593)
XLA Ops:
  0.0 0.8 copy.12
  0.8 1.0 copy.13
  1.7 1.6 fusion.3.w
  3.4 71.8 %shard_map.73 = (bf16[1040,1536]{1,0:T(8,128)(2,1)}, f32[1024,128]{1,0:T(8,128)}, bf16[2304,512]{1,0:T(8,128)(2,1)}) custom-call(bf16[128,2304]{1,0:T(8,128)(2,1)} %x.3, bf16[72,2304]{1,0:T(8,128)(2,1)} %fusion.3.w), custom_call_target="tpu_custom_call" | custom-call | tf_op jit(solution)/shard_map/pallas_call | solution.py:353
  75.2 0.0 copy-start
  75.2 1.6 copy-done
  76.8 0.0 copy-start.3
  76.8 1.0 copy-done.3
  77.8 0.0 copy-start.5
  77.8 0.7 copy-done.5
  78.6 27.5 %shard_map.74 = (bf16[1024,512]{1,0:T(8,128)(2,1)S(1)}, bf16[1024,512]{1,0:T(8,128)(2,1)S(1)}, bf16[4,128,256]{2,1,0:T(8,128)(2,1)S(1)}) custom-call(bf16[1040,1536]{1,0:T(8,128)(2,1)} %get-tuple-element.11.proj, f32[1024,128]{1,0:T(8,128)S(1)} %copy-done.3, f32[1024,512]{1,0:T(8,128)S(1)} %copy-done, f32[4,1536]{1,0:T(4,128)S(1)} %bitcast.5), custom_call_target="tpu_custom_call" | custom-call | tf_op jit(solution)/shard_map/pallas_call | solution.py:124
  106.1 0.0 copy-start.1
  106.1 1.0 copy-done.1
  107.0 0.0 copy-start.2
  107.0 1.0 copy-done.2
  108.1 0.0 copy-start.4
  108.1 0.7 copy-done.4
  108.8 74.2 %shard_map.75 = bf16[128,2304]{1,0:T(8,128)(2,1)} custom-call(bf16[1024,512]{1,0:T(8,128)(2,1)} %copy-done.1, bf16[1024,512]{1,0:T(8,128)(2,1)} %copy-done.2, bf16[4,128,256]{2,1,0:T(8,128)(2,1)} %copy-done.4, f32[1,128]{1,0:T(1,128)} %bitcast.9, bf16[2304,512]{1,0:T(8,128)(2,1)} %get-tuple-element.16.wo), custom_call_target="tpu_custom_call" | custom-call | tf_op jit(solution)/shard_map/pallas_call | solution.py:520
  183.0 1.9 %copy.15 = bf16[128,2304]{1,0:T(8,128)(2,1)} copy(bf16[128,2304]{1,0:T(8,128)(2,1)} %shard_map.75) | data formatting | bytes 1179648
Async XLA Ops:
  75.2 1.6 copy-start
  76.8 1.0 copy-start.3
  77.8 0.7 copy-start.5
  106.1 1.0 copy-start.1
  107.0 1.0 copy-start.2
  108.1 0.7 copy-start.4

commit v2 on v1

v2 whole, which is shorter than its diff:
```python
import functools
import jax
import jax.numpy as jnp
from jax import lax
from jax.experimental import pallas as pl
from jax.experimental.pallas import tpu as pltpu
from jax.sharding import PartitionSpec as P

f32, bf16 = jnp.float32, jnp.bfloat16
CH = 128
HD = 128


def mm(a, b):
    return jnp.dot(a.astype(bf16), b.astype(bf16), preferred_element_type=f32)


def mm_nt(a, b):
    return lax.dot_general(a.astype(bf16), b.astype(bf16), (((1,), (1,)), ((), ())), preferred_element_type=f32)


def mm_tn(a, b):
    return lax.dot_general(a.astype(bf16), b.astype(bf16), (((0,), (0,)), ((), ())), preferred_element_type=f32)


def chunk_terms(heads, chunks, load_proj, load_gate, strength, taps):
    row = lax.broadcasted_iota(jnp.int32, (CH, CH), 0)
    col = lax.broadcasted_iota(jnp.int32, (CH, CH), 1)
    incl, strict = row >= col, row > col
    lower = incl.astype(bf16)
    each = range(heads * chunks)
    width = heads * HD

    def conv(part, h):
        at = part * width + (h % heads) * HD
        p = load_proj(h // heads, at).astype(f32)
        y = taps[3:4, at:at + HD] * p[16:]
        for j in range(3):
            y = y + taps[j:j + 1, at:at + HD] * p[13 + j:13 + j + CH]
        return y * (0.5 + 0.5 * jnp.tanh(0.5 * y))

    def unit(m):
        return m * lax.rsqrt(jnp.sum(m * m, axis=-1, keepdims=True) + 1e-6)

    q = [unit(conv(0, h)) for h in each]
    k = [unit(conv(1, h)) for h in each]
    v = [conv(2, h) for h in each]
    b = [strength[h // heads][:, h % heads:h % heads + 1] for h in each]
    g = [load_gate(h // heads, h % heads) for h in each]
    ghi = [m.astype(bf16) for m in g]
    glo = [(g[h] - ghi[h].astype(f32)).astype(bf16) for h in each]
    cum = [mm(lower, ghi[h]) + mm(lower, glo[h]) for h in each]
    mid = [m[CH // 2 - 1:CH // 2] for m in cum]
    fin = [m[CH - 1:CH] for m in cum]
    up = [jnp.exp(cum[h] - mid[h]) for h in each]
    down = [jnp.exp(mid[h] - cum[h]) for h in each]
    emid = [jnp.exp(mid[h]) for h in each]
    k_up = [k[h] * up[h] for h in each]
    q_up = [q[h] * up[h] for h in each]
    k_down = [k[h] * down[h] for h in each]
    k_end = [k_down[h] * jnp.exp(fin[h] - mid[h]) for h in each]
    both = [mm_nt(jnp.concatenate([k_up[h], q_up[h]], axis=0), k_down[h]) for h in each]
    mix = [jnp.where(strict, b[h] * both[h][:CH], 0.0).astype(bf16) for h in each]
    score = [jnp.where(incl, both[h][CH:], 0.0).astype(bf16) for h in each]
    zero = jnp.zeros((CH, CH), bf16)

    def off(n):
        return ((row // (2 * n)) == (col // (2 * n))) & ((row // n) % 2 == 1) & ((col // n) % 2 == 0)

    near = (row // 16) == (col // 16)
    flat = []
    for h in each:
        m = jnp.where(near, mix[h].astype(f32), 0.0)
        total = m[0:16]
        for r in range(16, CH, 16):
            total = total + m[r:r + 16]
        flat.append(total.astype(bf16))
    flat = jnp.concatenate(flat, axis=0)
    row16 = lax.broadcasted_iota(jnp.int32, (16, CH), 0)
    col16 = lax.broadcasted_iota(jnp.int32, (16, CH), 1)
    small = [(row16 == col16 % 16).astype(f32) for h in each]
    for j in range(15):
        spread = mm(flat, near & ((row % 16) == j))
        small = [small[h] - spread[16 * h:16 * h + 16] * small[h][j:j + 1] for h in each]
    inv = [jnp.where(near, jnp.concatenate([small[h]] * (CH // 16), axis=0), 0.0) for h in each]
    n = 16
    while n < CH:
        m = off(n)
        part = [jnp.where(m, mix[h], zero) for h in each]
        low = [inv[h].astype(bf16) for h in each]
        step = [mm(part[h], low[h]).astype(bf16) for h in each]
        inv = [inv[h] - mm(low[h], step[h]) for h in each]
        n *= 2
    q_dec = [q_up[h] * emid[h] for h in each]
    rhs = [jnp.concatenate([b[h] * (k_up[h] * emid[h]), b[h] * v[h]], axis=1).astype(bf16) for h in each]
    wu = [mm(inv[h], rhs[h]).astype(bf16) for h in each]
    sw = [mm(score[h], wu[h]) for h in each]
    kw = [mm_tn(k_end[h], wu[h]) for h in each]
    reader = [q_dec[h] - sw[h][:, :HD] for h in each]
    local = [sw[h][:, HD:] for h in each]
    erase = [kw[h][:, :HD] for h in each]
    inject = [kw[h][:, HD:] for h in each]
    final = [jnp.sum(jnp.where(row == col, jnp.exp(fin[h]), 0.0), axis=1, keepdims=True) for h in each]
    return reader, local, erase, inject, final


MESH = pl.DeviceIdType.MESH
XN, YN = 4, 4
SEQ, TEN = 32, 8
PIECE = 72
PAIR = 2 * PIECE
COLS = 2304
HALF = COLS // 2
HEADS = 4
WIDTH = HEADS * HD
BETA_AT = 1536
OUT_AT = 1792


def place():
    s, z = lax.axis_index("seq"), lax.axis_index("tensor")
    core, chip = s % 2, s // 2
    return s, z, core, chip // YN, chip % YN


def remote(src, dst, ssem, rsem, to):
    copy = pltpu.make_async_remote_copy(src_ref=src, dst_ref=dst, send_sem=ssem, recv_sem=rsem, device_id=to, device_id_type=MESH)
    return copy


def greet(peers):
    barrier = pltpu.get_barrier_semaphore()
    for peer in peers:
        pl.semaphore_signal(barrier, inc=1, device_id=peer, device_id_type=MESH)
    pl.semaphore_wait(barrier, len(peers))


def layer_body(x, w, gate_in, taps, gain, out,
               xg, wf, wo, sib, blk, rim, proj, logit, gate, rdr, loc, ers, inj, fin, pbs, run, pb, rd, lo,
               sibpb, gy, pre, gx, ss_, sb, sin, nrm, part, rsend, rrecv,
               xs, xr, ws, wr, ss, sr, ps, pr, ls, csem, ysem, xsem, rssem, rrsem):
    s, z, core, cx, cy = place()
    a = jnp.where(core == 0, cx, cy)
    b = jnp.where(core == 0, cy, cx)

    def chip_of(da, db):
        ra, rb = (a + da) % 4, (b + db) % 4
        return jnp.where(core == 0, ra * YN + rb, rb * YN + ra)

    def dev_of(da, db):
        return (chip_of(da, db) * 2 + core, z)

    other = (s + 1 - 2 * core, z)
    right, left = (s, (z + 1) % TEN), (s, (z + TEN - 1) % TEN)
    after, before = ((s + 1) % SEQ, z), ((s + SEQ - 1) % SEQ, z)
    def y_dev(k):
        return ((cx * YN + (cy + k) % YN) * 2 + core, z)

    def x_dev(k):
        return ((((cx + k) % XN) * YN + cy) * 2 + core, z)

    greet([other, right, left, after, before] + [y_dev(k) for k in (1, 2, 3)] + [x_dev(k) for k in (1, 2, 3)])

    pair = remote(w, sib, ps.at[0], pr.at[0], other)
    pair.start()
    own = pltpu.make_async_copy(x, xg.at[z], ls.at[0])
    own.start()
    decay = pltpu.make_async_copy(gate_in, gate, ls.at[1])
    decay.start()

    def x_copy(d, k):
        c = (z + (TEN - k + 1 if d == 0 else k - 1)) % TEN
        if k == 4:
            here = xg.at[c, pl.ds(64 * d, 64)]
        else:
            here = xg.at[c]
        return remote(x if k == 1 else here, here, xs.at[d, k - 1], xr.at[d, k - 1], right if d == 0 else left)

    def x_recv(d, k):
        c = (z + (TEN - k if d == 0 else k)) % TEN
        here = xg.at[c, pl.ds(64 * d, 64)] if k == 4 else xg.at[c]
        return remote(here, here, xs.at[d, k - 1], xr.at[d, k - 1], right if d == 0 else left)

    for d in range(2):
        x_copy(d, 1).start()

    pair.wait_recv()
    mine = w[...].astype(f32)
    theirs = sib[...].astype(f32)
    blk[0:PIECE] = jnp.where(core == 0, mine, theirs)
    blk[PIECE:PAIR] = jnp.where(core == 0, theirs, mine)
    here = pl.multiple_of(chip_of(0, 0) * PAIR, 16)
    wf[pl.ds(here, PAIR)] = blk[:, :OUT_AT].astype(bf16)
    wo[pl.ds(here, PAIR)] = blk[:, OUT_AT:].astype(bf16)

    def w_ref(g, da, db, who=core):
        full, n = (wf, OUT_AT // 2) if g == 0 else (wo, (COLS - OUT_AT) // 2)
        rows = pl.ds(pl.multiple_of(chip_of(da, db) * PAIR, 16), PAIR)
        return full.at[rows, pl.ds(pl.multiple_of(who * n, 128), n)]

    sends = []
    used = [0, 0]

    def w_send(g, da, db, ta, tb):
        ra, rb = (da - ta) % 4, (db - tb) % 4
        n = used[g]
        used[g] += 1

        def copy():
            ref = w_ref(g, da, db)
            return remote(ref, ref, ws.at[g, n], wr.at[g, ra * 4 + rb], dev_of(ta, tb))

        copy().start()
        sends.append(copy)

    def w_wait(g, da, db):
        ref = w_ref(g, da, db)
        remote(ref, ref, ws.at[g, 0], wr.at[g, da * 4 + db], other).wait_recv()

    def across(g, da, db):
        def copy():
            ref = w_ref(g, da, db)
            return remote(ref, ref, ss.at[g, da * 4 + db], sr.at[g, da * 4 + db], other)

        copy().start()
        sends.append(copy)

    def hop_b(g, da):
        w_send(g, da, 0, 0, 1)
        w_send(g, da, 0, 0, 3)

    def first_hops(g):
        w_send(g, 0, 0, 1, 0)
        w_send(g, 0, 0, 3, 0)
        hop_b(g, 0)

    def relay_hops(g, blocks):
        for da, db in blocks:
            w_wait(g, da, db)
            if (da, db) == (3, 0):
                w_send(g, da, db, 1, 0)
            if db == 0:
                hop_b(g, da)
            if (db == 3 and da < 2) or (db == 1 and da > 1):
                w_send(g, da, db, 0, 1 if db == 3 else 3)
            across(g, da, db)

    def other_half(g):
        for i in range(1, 16):
            ref = w_ref(g, i % 4, i // 4, 1 - core)
            remote(ref, ref, ss.at[g, i], sr.at[g, i], other).wait_recv()

    def x_forward(k):
        for d in range(2):
            x_recv(d, k).wait_recv()
            x_copy(d, k + 1).start()

    near_blocks = [(3, 0), (1, 0), (2, 0), (0, 3), (0, 1)]
    side_blocks = [(3, 1), (1, 3), (3, 3), (1, 1)]
    far_blocks = [(2, 1), (2, 3), (0, 2), (3, 2), (1, 2), (2, 2)]
    first_hops(0)
    relay_hops(0, near_blocks)
    x_forward(1)
    relay_hops(0, side_blocks)
    relay_hops(0, far_blocks)
    first_hops(1)
    x_forward(2)
    other_half(0)
    own.wait()
    decay.wait()

    rim_copy = remote(proj.at[pl.ds(TEN * CH, 16)], rim, ps.at[1], pr.at[1], after)

    @pl.when(s == 0)
    def _():
        proj[0:16] = jnp.zeros((16, BETA_AT), bf16)

    def project(c):
        r = pl.multiple_of(16 + c * CH, 16)

        def tile(n, carry):
            at = pl.multiple_of(n * 768, 256)
            acc = jnp.dot(xg[c], wf[:, pl.ds(at, 768)], preferred_element_type=f32)
            proj[pl.ds(r, CH), pl.ds(at, 768)] = acc.astype(bf16)
            return carry

        lax.fori_loop(0, BETA_AT // 768, tile, 0)
        logit[pl.ds(pl.multiple_of(c * CH, CH), CH)] = jnp.dot(xg[c], wf[:, BETA_AT:BETA_AT + 128], preferred_element_type=f32)

        @pl.when((c == TEN - 1) & (s < SEQ - 1))
        def _():
            rim_copy.start()

    def terms(k):
        chunks = [(z + TEN - k) % TEN, (z + k + 1) % TEN]
        at = [pl.multiple_of(c * CH, CH) for c in chunks]

        @pl.when((s > 0) & ((chunks[0] == 0) | (chunks[1] == 0)))
        def _():
            rim_copy.wait_recv()
            proj[0:16] = rim[...]

        reader, local, erase, inject, final = chunk_terms(
            HEADS, 2,
            lambda i, col: proj[pl.ds(at[i], CH + 16), col:col + HD],
            lambda i, h: gate[pl.ds(at[i], CH), h * HD:(h + 1) * HD],
            [1.0 / (1.0 + jnp.exp(-logit[pl.ds(at[i], CH)])) for i in range(2)],
            taps)
        for i in range(2):
            for h in range(HEADS):
                n = i * HEADS + h
                rdr[chunks[i], h] = reader[n].astype(bf16)
                loc[chunks[i], h] = local[n]
                ers[chunks[i], h] = erase[n].astype(bf16)
                inj[chunks[i], h] = inject[n]
                fin[chunks[i], h] = final[n]

    project(z)

    def step(k, carry):
        @pl.when(k == 2)
        def _():
            x_forward(3)

        @pl.when(k < 3)
        def _():
            def one(i, carry):
                project((z + jnp.where(i == 0, TEN - 1 - k, k + 1)) % TEN)
                return carry
            lax.fori_loop(0, 2, one, 0)

        @pl.when(k == 3)
        def _():
            for d in range(2):
                x_recv(d, 4).wait_recv()
            project((z + 4) % TEN)

        for n, blocks in enumerate((near_blocks, side_blocks, far_blocks)):
            @pl.when(k == n)
            def _():
                relay_hops(1, blocks)

        terms(k)
        return carry

    lax.fori_loop(0, 4, step, 0)
    other_half(1)

    eye2 = (lax.broadcasted_iota(jnp.int32, (HD, 2 * HD), 0) == lax.broadcasted_iota(jnp.int32, (HD, 2 * HD), 1)).astype(bf16)
    zeros = jnp.zeros((HD, HD), f32)
    for h in range(HEADS):
        run[h] = eye2.astype(f32)

    def fold(c, carry):
        for h in range(HEADS):
            now = run[h]
            short = now.astype(bf16)
            pbs[c, h] = short
            run[h] = fin[c, h] * now - mm(ers[c, h], short) + jnp.concatenate([zeros, inj[c, h]], axis=1)
        return carry

    lax.fori_loop(0, TEN, fold, 0)
    for h in range(HEADS):
        pb[h] = run[h].astype(bf16)

    def unfold(c, carry):
        r = pl.ds(pl.multiple_of(c * CH, CH), CH)
        for h in range(HEADS):
            both = mm(rdr[c, h], pbs[c, h])
            rd[r, h * HD:(h + 1) * HD] = both[:, :HD].astype(bf16)
            lo[r, h * HD:(h + 1) * HD] = both[:, HD:] + loc[c, h]
        return carry

    mine0, their0 = 2 * core, 2 - 2 * core
    first = remote(pb.at[pl.ds(their0, 2)], sibpb, csem.at[0], csem.at[1], other)
    first.start()

    def chain(later, earlier):
        p = mm(later[:, :HD], earlier)
        return p + jnp.concatenate([jnp.zeros((HD, HD), f32), later[:, HD:].astype(f32)], axis=1)

    first.wait_recv()
    heads = range(2)
    lead = []
    for i in heads:
        own, got = pb[mine0 + i], sibpb[i]
        head, tail = jnp.where(core == 0, own, got), jnp.where(core == 0, got, own)
        lead.append(head)
        gy[cy, i] = chain(tail, head).astype(bf16)
    y_copies = [remote(gy.at[cy], gy.at[cy], ysem.at[0, k], ysem.at[1, k], y_dev(k)) for k in (1, 2, 3)]
    for copy in y_copies:
        copy.start()
    lax.fori_loop(0, TEN, unfold, 0)
    for k in (1, 2, 3):
        slot = gy.at[(cy + YN - k) % YN]
        remote(slot, slot, ysem.at[0, k], ysem.at[1, k], y_dev(k)).wait_recv()
    acc = [gy[0, i] for i in heads]
    for i in heads:
        pre[0, i] = eye2
        pre[1, i] = acc[i]
    for k in (1, 2, 3):
        acc = [chain(gy[k, i], acc[i]).astype(bf16) for i in heads]
        for i in heads:
            if k < 3:
                pre[k + 1, i] = acc[i]
            else:
                gx[cx, i] = acc[i]
    x_copies = [remote(gx.at[cx], gx.at[cx], xsem.at[0, k], xsem.at[1, k], x_dev(k)) for k in (1, 2, 3)]
    for copy in x_copies:
        copy.start()
    for k in (1, 2, 3):
        slot = gx.at[(cx + XN - k) % XN]
        remote(slot, slot, xsem.at[0, k], xsem.at[1, k], x_dev(k)).wait_recv()
    state = [jnp.zeros((HD, HD), f32) for i in heads]
    for i in heads:
        ss_[0, i] = state[i]
    for k in range(3):
        state = [mm(gx[k, i, :, :HD], state[i]) + gx[k, i, :, HD:].astype(f32) for i in heads]
        for i in heads:
            ss_[k + 1, i] = state[i]
    for i in heads:
        entry = mm(pre[cy, i, :, :HD], ss_[cx, i]) + pre[cy, i, :, HD:].astype(f32)
        behind = mm(lead[i][:, :HD], entry) + lead[i][:, HD:].astype(f32)
        sin[mine0 + i] = jnp.where(core == 0, entry, behind).astype(bf16)
        sb[i] = jnp.where(core == 0, behind, entry).astype(bf16)
    last = remote(sb, sin.at[pl.ds(mine0, 2)], csem.at[2], csem.at[3], other)
    last.start()
    their = sin.at[pl.ds(their0, 2)]
    remote(their, their, csem.at[2], csem.at[3], other).wait_recv()

    def attend(c):
        r = pl.ds(pl.multiple_of(c * CH, CH), CH)
        att = [mm(rd[r, h * HD:(h + 1) * HD], sin[h]) + lo[r, h * HD:(h + 1) * HD] for h in range(4)]
        for h in range(4):
            scale = lax.rsqrt(jnp.mean(att[h] * att[h], axis=-1, keepdims=True) + 1e-5)
            nrm[c, :, h * HD:(h + 1) * HD] = (att[h] * scale * gain[...]).astype(bf16)

    def partial(d, c):
        for n in range(0, HALF, 384):
            part[d, :, n:n + 384] = mm_nt(nrm[c], wo[d * HALF + n:d * HALF + n + 384])

    def chunk(d, t):
        return (z + (2 * TEN - 1 - t if d == 0 else 1 + t)) % TEN

    def send(d, t, u):
        rows = pl.ds(u * 64, 64)
        return remote(rsend.at[d, t, rows], rrecv.at[d, t, rows], rssem.at[d, t, u], rrsem.at[d, t, u], right if d == 0 else left)

    for d in range(2):
        c = chunk(d, 0)
        attend(c)
        partial(d, c)
        for u in range(2):
            rsend[d, 0, u * 64:u * 64 + 64] = part[d, u * 64:u * 64 + 64].astype(bf16)
            send(d, 0, u).start()

    def ring(t, carry):
        for d in range(2):
            c = chunk(d, t)

            @pl.when((t < 3) | ((t == 3) & (d == 0)))
            def _():
                attend(c)

            partial(d, c)
        for u in range(2):
            for d in range(2):
                send(d, t - 1, u).wait_recv()
                total = part[d, u * 64:u * 64 + 64] + rrecv[d, t - 1, u * 64:u * 64 + 64].astype(f32)
                rsend[d, t, u * 64:u * 64 + 64] = total.astype(bf16)
                send(d, t, u).start()
        return carry

    lax.fori_loop(1, 7, ring, 0)
    attend(z)
    for d in range(2):
        partial(d, z)
    for u in range(2):
        for d in range(2):
            send(d, 6, u).wait_recv()
            total = part[d, u * 64:u * 64 + 64] + rrecv[d, 6, u * 64:u * 64 + 64].astype(f32)
            out[u * 64:u * 64 + 64, d * HALF:(d + 1) * HALF] = total.astype(bf16)

    @pl.when(s < SEQ - 1)
    def _():
        rim_copy.wait_send()

    pair.wait_send()
    for copy in sends:
        copy().wait_send()
    for d in range(2):
        for k in range(1, 5):
            x_copy(d, k).wait_send()
    first.wait_send()
    last.wait_send()
    for copy in y_copies + x_copies:
        copy.wait_send()

    def drain(t, carry):
        for d in range(2):
            for u in range(2):
                send(d, t, u).wait_send()
        return carry

    lax.fori_loop(0, 7, drain, 0)


def layer(x, w, gate, taps, gain):
    vm, dma = pltpu.VMEM, pltpu.SemaphoreType.DMA
    whole = pl.BlockSpec(memory_space=pltpu.VMEM)
    return pl.pallas_call(
        layer_body,
        in_specs=[whole, whole, pl.BlockSpec(memory_space=pl.ANY), whole, whole],
        out_specs=whole,
        out_shape=jax.ShapeDtypeStruct((CH, COLS), bf16),
        scratch_shapes=[
            vm((TEN, CH, COLS), bf16),
            vm((COLS, OUT_AT), bf16),
            vm((COLS, WIDTH), bf16),
            vm((PIECE, COLS), bf16),
            vm((PAIR, COLS), f32),
            vm((16, BETA_AT), bf16),
            vm((TEN * CH + 16, BETA_AT), bf16),
            vm((TEN * CH, 128), f32),
            vm((TEN * CH, WIDTH), f32),
            vm((TEN, HEADS, CH, HD), bf16),
            vm((TEN, HEADS, CH, HD), f32),
            vm((TEN, HEADS, HD, HD), bf16),
            vm((TEN, HEADS, HD, HD), f32),
            vm((TEN, HEADS, HD, 1), f32),
            vm((TEN, HEADS, HD, 2 * HD), bf16),
            vm((HEADS, HD, 2 * HD), f32),
            vm((HEADS, HD, 2 * HD), bf16),
            vm((TEN * CH, WIDTH), bf16),
            vm((TEN * CH, WIDTH), f32),
            vm((2, HD, 2 * HD), bf16),
            vm((YN, 2, HD, 2 * HD), bf16),
            vm((YN, 2, HD, 2 * HD), bf16),
            vm((XN, 2, HD, 2 * HD), bf16),
            vm((XN, 2, HD, HD), f32),
            vm((2, HD, HD), bf16),
            vm((4, HD, HD), bf16),
            vm((TEN, CH, WIDTH), bf16),
            vm((2, CH, HALF), f32),
            vm((2, 7, CH, HALF), bf16),
            vm((2, 7, CH, HALF), bf16),
            dma((2, 4)), dma((2, 4)), dma((2, 16)), dma((2, 16)), dma((2, 16)), dma((2, 16)),
            dma((2,)), dma((2,)), dma((2,)), dma((4,)), dma((2, 4)), dma((2, 4)), dma((2, 7, 2)), dma((2, 7, 2)),
        ],
        compiler_params=pltpu.CompilerParams(collective_id=0, has_side_effects=True, vmem_limit_bytes=62 << 20),
    )(x, w, gate, taps, gain)


def per_device(x_rows, w_qkv, w_beta, conv_weight, log_decay, norm_gain, w_out):
    packed = jnp.concatenate(
        [w_qkv.reshape(PIECE, BETA_AT), jnp.pad(w_beta, ((0, 0), (0, OUT_AT - BETA_AT - w_beta.shape[1]))), w_out.T], axis=1)
    return layer(x_rows, packed, log_decay, conv_weight.reshape(4, BETA_AT), norm_gain.reshape(1, HD))


def solution(mesh):
    in_specs = (
        P(("seq", "tensor"), None),
        P("seq", None, "tensor"),
        P("seq", "tensor"),
        P(None, None, "tensor"),
        P("seq", "tensor"),
        P(),
        P("tensor", "seq"),
    )
    return jax.shard_map(per_device, mesh=mesh, in_specs=in_specs, out_specs=P(("seq", "tensor"), None), check_vma=False)
```

time: 185 us -> 155 us (0.84)
  Pallas kernels: 174 us -> 149 us
  local copies, waits for them, and re-layouts: 9.71 us -> 3.66 us
    pallas_call x3 -> x1, Pallas kernels: 174 us -> 149 us  [layer(): pl.pallas_call(layer_body, in_specs=[whole, whole, pl.BlockSpec(memory_sp...]
    unnamed x14 -> x2, local copies, waits for them, and re-layouts: 8.76 us -> 2.7 us
where the time goes in v2:
time: 155 us; the launch traced here: 154 us
  Pallas kernels  149 us (96%)
  local copies, waits for them, and re-layouts  3.66 us (2%)
  other arithmetic  1.64 us (1%)
    pallas_call x1, Pallas kernels, layer(): pl.pallas_call(layer_body, in_specs=[whole, whole, pl.BlockSpec(memory_sp...  149 us

profile of v2, /device:TPU:1, one launch (start us, length us, event | category | flops | bytes accessed | tf_op | source)
XLA Modules:
  0.0 154.3 jit_solution(13573478078532138477)
XLA Ops:
  0.0 0.8 copy.12
  0.8 1.0 copy.13
  1.7 1.6 %fusion.3.w = bf16[72,2304]{1,0:T(8,128)(2,1)} fusion(bf16[72,4]{1,0:T(8,128)(2,1)S(1)} %copy.12, bf16[72,512]{1,0:T(8,128)(2,1)} %bitcast.7, bf16[72,1536]{1,0:T(8,128)(2,1)S(1)} %bitcast.5), kind=kLoop, calls=%fused_computation.5 | loop fusion | flops 1658880 | bytes 627264 | tf_op jit(solution)/shard_map/concatenate | solution.py:555
  3.4 149.0 %shard_map.73 = bf16[128,2304]{1,0:T(8,128)(2,1)} custom-call(bf16[128,2304]{1,0:T(8,128)(2,1)} %x.3, bf16[72,2304]{1,0:T(8,128)(2,1)} %fusion.3.w, f32[1024,512]{1,0:T(8,128)} %gate_in.1, f32[4,1536]{1,0:T(4,128)} %bitcast.8, f32[1,128]{1,0:T(1,128)} %bitcast.9), custom_call_target="tpu_custom_call" | custom-call | tf_op jit(solution)/shard_map/pallas_call | solution.py:511
  152.4 1.9 %copy.15 = bf16[128,2304]{1,0:T(8,128)(2,1)} copy(bf16[128,2304]{1,0:T(8,128)(2,1)} %shard_map.73) | data formatting | bytes 1179648

commit v3 on v2

v3 whole, which is shorter than its diff:
```python
import functools
import jax
import jax.numpy as jnp
from jax import lax
from jax.experimental import pallas as pl
from jax.experimental.pallas import tpu as pltpu
from jax.sharding import PartitionSpec as P

f32, bf16 = jnp.float32, jnp.bfloat16
CH = 128
HD = 128


def mm(a, b):
    return jnp.dot(a.astype(bf16), b.astype(bf16), preferred_element_type=f32)


def mm_nt(a, b):
    return lax.dot_general(a.astype(bf16), b.astype(bf16), (((1,), (1,)), ((), ())), preferred_element_type=f32)


def mm_tn(a, b):
    return lax.dot_general(a.astype(bf16), b.astype(bf16), (((0,), (0,)), ((), ())), preferred_element_type=f32)


def triangle():
    row = lax.broadcasted_iota(jnp.int32, (CH, CH), 0)
    col = lax.broadcasted_iota(jnp.int32, (CH, CH), 1)
    return row, col


def short_conv(p, taps, at):
    p = p.astype(f32)
    y = taps[3:4, at:at + HD] * p[16:]
    for j in range(3):
        y = y + taps[j:j + 1, at:at + HD] * p[13 + j:13 + j + CH]
    return y * (0.5 + 0.5 * jnp.tanh(0.5 * y))


def unit(m):
    return m * lax.rsqrt(jnp.sum(m * m, axis=-1, keepdims=True) + 1e-6)


def unit_lower_inverse(mix):
    row, col = triangle()
    each = range(len(mix))
    near = (row // 16) == (col // 16)
    flat = []
    for h in each:
        m = jnp.where(near, mix[h].astype(f32), 0.0)
        total = m[0:16]
        for r in range(16, CH, 16):
            total = total + m[r:r + 16]
        flat.append(total.astype(bf16))
    flat = jnp.concatenate(flat, axis=0)
    row16 = lax.broadcasted_iota(jnp.int32, (16, CH), 0)
    col16 = lax.broadcasted_iota(jnp.int32, (16, CH), 1)
    small = [(row16 == col16 % 16).astype(f32) for h in each]
    for j in range(15):
        spread = mm(flat, near & ((row % 16) == j))
        small = [small[h] - spread[16 * h:16 * h + 16] * small[h][j:j + 1] for h in each]
    inv = [jnp.where(near, jnp.concatenate([small[h]] * (CH // 16), axis=0), 0.0) for h in each]
    zero = jnp.zeros((CH, CH), bf16)
    n = 16
    while n < CH:
        off = ((row // (2 * n)) == (col // (2 * n))) & ((row // n) % 2 == 1) & ((col // n) % 2 == 0)
        part = [jnp.where(off, mix[h], zero) for h in each]
        low = [inv[h].astype(bf16) for h in each]
        step = [mm(part[h], low[h]).astype(bf16) for h in each]
        inv = [inv[h] - mm(low[h], step[h]) for h in each]
        n *= 2
    return [inv[h].astype(bf16) for h in each]


def key_terms(keys, strength, decay):
    row, col = triangle()
    lower = (row >= col).astype(bf16)
    each = range(len(keys))
    k = [unit(m) for m in keys]
    ghi = [m.astype(bf16) for m in decay]
    glo = [(decay[h] - ghi[h].astype(f32)).astype(bf16) for h in each]
    cum = [mm(lower, ghi[h]) + mm(lower, glo[h]) for h in each]
    mid = [m[CH // 2 - 1:CH // 2] for m in cum]
    fin = [m[CH - 1:CH] for m in cum]
    rel = [cum[h] - mid[h] for h in each]
    k_up = [k[h] * jnp.exp(rel[h]) for h in each]
    k_down = [k[h] * jnp.exp(-rel[h]) for h in each]
    k_end = [(k_down[h] * jnp.exp(fin[h] - mid[h])).astype(bf16) for h in each]
    k_down = [m.astype(bf16) for m in k_down]
    mix = [mm_nt(k_up[h], k_down[h]) for h in each]
    mix = [jnp.where(row > col, strength[h] * mix[h], 0.0).astype(bf16) for h in each]
    inv = unit_lower_inverse(mix)
    emid = [jnp.exp(m) for m in mid]
    w = [mm(inv[h], strength[h] * (k_up[h] * emid[h])).astype(bf16) for h in each]
    erase = [mm_tn(k_end[h], w[h]).astype(bf16) for h in each]
    final = [jnp.sum(jnp.where(row == col, jnp.exp(fin[h]), 0.0), axis=1, keepdims=True) for h in each]
    return rel, emid, k_down, k_end, inv, w, erase, final


def value_terms(values, strength, k_end, inv):
    each = range(len(values))
    u = [mm(inv[h], strength[h] * values[h]).astype(bf16) for h in each]
    inject = [mm_tn(k_end[h], u[h]) for h in each]
    return u, inject


def read_terms(query, rel, emid, k_down, w, u):
    row, col = triangle()
    each = range(len(query))
    q = [unit(query[h]) * jnp.exp(rel[h]) for h in each]
    score = [jnp.where(row >= col, mm_nt(q[h], k_down[h]), 0.0).astype(bf16) for h in each]
    sw = [mm(score[h], jnp.concatenate([w[h], u[h]], axis=1)) for h in each]
    reader = [(q[h] * emid[h] - sw[h][:, :HD]).astype(bf16) for h in each]
    local = [sw[h][:, HD:] for h in each]
    return reader, local


MESH = pl.DeviceIdType.MESH
XN, YN = 4, 4
SEQ, TEN = 32, 8
PIECE = 72
PAIR = 2 * PIECE
COLS = 2304
HALF = COLS // 2
HEADS = 4
WIDTH = HEADS * HD
QKV = 1536
BETA_AT = 512
V_AT = 768
Q_AT = 1280
OUT_AT = 1792


def place():
    s, z = lax.axis_index("seq"), lax.axis_index("tensor")
    core, chip = s % 2, s // 2
    return s, z, core, chip // YN, chip % YN


def remote(src, dst, ssem, rsem, to):
    copy = pltpu.make_async_remote_copy(src_ref=src, dst_ref=dst, send_sem=ssem, recv_sem=rsem, device_id=to, device_id_type=MESH)
    return copy


def greet(peers):
    barrier = pltpu.get_barrier_semaphore()
    for peer in peers:
        pl.semaphore_signal(barrier, inc=1, device_id=peer, device_id_type=MESH)
    pl.semaphore_wait(barrier, len(peers))


def layer_body(x, w_qkv, w_beta, w_out, gate_in, taps, gain, out,
               xg, wf, w, sib, blk, rim, proj, logit, gate, emid, kdn, ken, inv, wk, uv, rdr, loc, ers, inj, fin, pbs, run, pb, rd, lo,
               gc, pre, gx, begin, sb, sin, nrm, part, rsend, rrecv,
               xs, xr, ws, wr, ss, sr, ps, pr, ls, upsem, xsem, downsem, rssem, rrsem):
    s, z, core, cx, cy = place()
    a = jnp.where(core == 0, cx, cy)
    b = jnp.where(core == 0, cy, cx)

    def chip_of(da, db):
        ra, rb = (a + da) % 4, (b + db) % 4
        return jnp.where(core == 0, ra * YN + rb, rb * YN + ra)

    def dev_of(da, db):
        return (chip_of(da, db) * 2 + core, z)

    other = (s + 1 - 2 * core, z)
    right, left = (s, (z + 1) % TEN), (s, (z + TEN - 1) % TEN)
    after, before = ((s + 1) % SEQ, z), ((s + SEQ - 1) % SEQ, z)
    def column_dev(i):
        return ((cx * YN + i // 2) * 2 + i % 2, z)

    def x_dev(k):
        return ((((cx + k) % XN) * YN + cy) * 2 + core, z)

    me = cy * 2 + core
    greet([right, left, after, before] + [x_dev(k) for k in (1, 2, 3)] + [column_dev((me + k) % 8) for k in range(1, 8)])

    def x_copy(d, k, i):
        c, r = (z + (TEN - k + 1 if d == 0 else k - 1)) % TEN, pl.ds(64 * i, 64)
        here = xg.at[c, r]
        return remote(x.at[r] if k == 1 else here, here, xs.at[d, k - 1, i], xr.at[d, k - 1, i], right if d == 0 else left)

    def x_recv(d, k, i):
        here = xg.at[(z + (TEN - k if d == 0 else k)) % TEN, pl.ds(64 * i, 64)]
        return remote(here, here, xs.at[d, k - 1, i], xr.at[d, k - 1, i], right if d == 0 else left)

    for i in range(2):
        for d in range(2):
            x_copy(d, 1, i ^ d).start()

    w[:, :BETA_AT] = w_qkv[1]
    spread = (lax.broadcasted_iota(jnp.int32, (HEADS, V_AT - BETA_AT), 0) == lax.broadcasted_iota(jnp.int32, (HEADS, V_AT - BETA_AT), 1))
    w[:, BETA_AT:V_AT] = mm_tn(w_beta[...], spread).astype(bf16)
    w[:, V_AT:Q_AT] = w_qkv[2]
    w[:, Q_AT:OUT_AT] = w_qkv[0]
    w[:, OUT_AT:] = w_out[...]
    pair = remote(w, sib, ps.at[0], pr.at[0], other)
    pair.start()
    own = pltpu.make_async_copy(x, xg.at[z], ls.at[0])
    own.start()
    decay = pltpu.make_async_copy(gate_in, gate, ls.at[1])
    decay.start()
    pair.wait_recv()
    mine = w[...].astype(f32)
    theirs = sib[...].astype(f32)
    blk[0:PIECE] = jnp.where(core == 0, mine, theirs)
    blk[PIECE:PAIR] = jnp.where(core == 0, theirs, mine)
    here = pl.multiple_of(chip_of(0, 0) * PAIR, 16)
    wf[pl.ds(here, PAIR)] = blk[...].astype(bf16)

    def w_ref(g, da, db, who=core):
        full, first, n = ((wf, 0, Q_AT // 2), (wf, Q_AT, (COLS - Q_AT) // 2))[g]
        rows = pl.ds(pl.multiple_of(chip_of(da, db) * PAIR, 16), PAIR)
        return full.at[rows, pl.ds(pl.multiple_of(first + who * n, 128), n)]

    sends = []
    used = [0] * 2

    def w_send(g, da, db, ta, tb):
        ra, rb = (da - ta) % 4, (db - tb) % 4
        n = used[g]
        used[g] += 1

        def copy():
            ref = w_ref(g, da, db)
            return remote(ref, ref, ws.at[g, n], wr.at[g, ra * 4 + rb], dev_of(ta, tb))

        copy().start()
        sends.append(copy)

    def w_wait(g, da, db):
        ref = w_ref(g, da, db)
        remote(ref, ref, ws.at[g, 0], wr.at[g, da * 4 + db], other).wait_recv()

    def across(g, da, db):
        def copy():
            ref = w_ref(g, da, db)
            return remote(ref, ref, ss.at[g, da * 4 + db], sr.at[g, da * 4 + db], other)

        copy().start()
        sends.append(copy)

    def hop_b(g, da):
        w_send(g, da, 0, 0, 1)
        w_send(g, da, 0, 0, 3)

    def first_hops(g):
        w_send(g, 0, 0, 1, 0)
        w_send(g, 0, 0, 3, 0)
        hop_b(g, 0)

    def relay_hops(g, blocks):
        for da, db in blocks:
            w_wait(g, da, db)
            if (da, db) == (3, 0):
                w_send(g, da, db, 1, 0)
            if db == 0:
                hop_b(g, da)
            if (db == 3 and da < 2) or (db == 1 and da > 1):
                w_send(g, da, db, 0, 1 if db == 3 else 3)
            across(g, da, db)

    def other_half(g):
        for i in range(1, 16):
            ref = w_ref(g, i % 4, i // 4, 1 - core)
            remote(ref, ref, ss.at[g, i], sr.at[g, i], other).wait_recv()

    def x_forward(k, i):
        for d in range(2):
            x_recv(d, k, i ^ d).wait_recv()
            if k < 3 or i == 0:
                x_copy(d, k + 1, i ^ d).start()

    rims = []
    for n in range(3):
        cols = pl.ds(n * WIDTH, WIDTH)
        rims.append(remote(proj.at[pl.ds(TEN * CH, 16), cols], rim.at[:, cols], ps.at[1 + n], pr.at[1 + n], after))

    @pl.when(s == 0)
    def _():
        proj[0:16] = jnp.zeros((16, QKV), bf16)

    def project(c, part):
        r = pl.multiple_of(16 + c * CH, 16)
        at = (0, V_AT, Q_AT)[part]
        acc = jnp.dot(xg[c], wf[:, at:at + WIDTH], preferred_element_type=f32)
        proj[pl.ds(r, CH), part * WIDTH:(part + 1) * WIDTH] = acc.astype(bf16)
        if part == 0:
            acc = jnp.dot(xg[c], wf[:, BETA_AT:BETA_AT + 128], preferred_element_type=f32)
            logit[pl.ds(pl.multiple_of(c * CH, CH), CH)] = acc

        @pl.when((c == TEN - 1) & (s < SEQ - 1))
        def _():
            rims[part].start()

    def pair_of(k):
        chunks = [(z + TEN - k) % TEN, (z + k + 1) % TEN]
        return chunks, [pl.multiple_of(c * CH, CH) for c in chunks], [(i, h) for i in range(2) for h in range(HEADS)]

    def rim_in(chunks, part):
        @pl.when((s > 0) & ((chunks[0] == 0) | (chunks[1] == 0)))
        def _():
            rims[part].wait_recv()
            proj[0:16, part * WIDTH:(part + 1) * WIDTH] = rim[:, part * WIDTH:(part + 1) * WIDTH]

    def strengths(at):
        b = [1.0 / (1.0 + jnp.exp(-logit[pl.ds(at[i], CH)])) for i in range(2)]
        return [b[i][:, h:h + 1] for i in range(2) for h in range(HEADS)]

    def conv(at, i, h, part):
        col, tap = part * WIDTH + h * HD, ((1, 2, 0)[part]) * WIDTH + h * HD
        return short_conv(proj[pl.ds(at[i], CH + 16), col:col + HD], taps, tap)

    def put(chunks, each, refs, got):
        for n, (i, h) in enumerate(each):
            for ref, value in zip(refs, got):
                ref[chunks[i], h] = value[n]

    def take(chunks, each, *refs):
        return [[ref[chunks[i], h] for i, h in each] for ref in refs]

    def decays(at, each):
        return [gate[pl.ds(at[i], CH), h * HD:(h + 1) * HD] for i, h in each]

    def keys_of(k):
        chunks, at, each = pair_of(k)
        rim_in(chunks, 0)
        got = key_terms([conv(at, i, h, 0) for i, h in each], strengths(at), decays(at, each))
        for n, (i, h) in enumerate(each):
            gate[pl.ds(at[i], CH), h * HD:(h + 1) * HD] = got[0][n]
        put(chunks, each, (emid, kdn, ken, inv, wk, ers, fin), got[1:])

    def values_of(k):
        chunks, at, each = pair_of(k)
        rim_in(chunks, 1)
        got = value_terms([conv(at, i, h, 1) for i, h in each], strengths(at), *take(chunks, each, ken, inv))
        put(chunks, each, (uv, inj), got)

    def reads_of(k):
        chunks, at, each = pair_of(k)
        rim_in(chunks, 2)
        got = read_terms([conv(at, i, h, 2) for i, h in each], decays(at, each), *take(chunks, each, emid, kdn, wk, uv))
        put(chunks, each, (rdr, loc), got)

    near_blocks = [(3, 0), (1, 0), (0, 3), (0, 1)]
    side_blocks = [(2, 0), (3, 1), (1, 3), (3, 3), (1, 1)]
    far_blocks = [(2, 1), (2, 3), (0, 2), (3, 2), (1, 2), (2, 2)]
    first_hops(0)
    x_forward(1, 0)
    relay_hops(0, near_blocks)
    first_hops(1)
    x_forward(1, 1)
    relay_hops(0, side_blocks)
    relay_hops(1, near_blocks)
    x_forward(2, 0)
    relay_hops(0, far_blocks)
    x_forward(2, 1)
    own.wait()
    decay.wait()
    other_half(0)

    def nth(n):
        return (z + TEN + jnp.where(n % 2 == 1, -((n + 1) // 2), n // 2)) % TEN

    def many(part, lo_n, hi_n):
        def one(n, carry):
            project(nth(n), part)
            return carry
        lax.fori_loop(lo_n, hi_n, one, 0)

    def pairs(f, lo_n, hi_n):
        def one(n, carry):
            f(n)
            return carry
        lax.fori_loop(lo_n, hi_n, one, 0)

    def step(t, carry):
        when = lambda n: pl.when(t == n)

        @when(2)
        def _():
            x_forward(3, 1)

        @when(3)
        def _():
            for d in range(2):
                x_recv(d, 4, d).wait_recv()

        lo_n = jnp.where(t == 0, 0, 2 * t + 1)
        hi_n = jnp.minimum(2 * t + 3, TEN)
        many(0, lo_n, hi_n)
        many(1, lo_n, hi_n)

        @when(0)
        def _():
            relay_hops(1, side_blocks)

        keys_of(t)
        values_of(t)

        @when(0)
        def _():
            x_forward(3, 0)

        @when(1)
        def _():
            relay_hops(1, far_blocks)

        return carry

    lax.fori_loop(0, 4, step, 0)

    eye2 = (lax.broadcasted_iota(jnp.int32, (HD, 2 * HD), 0) == lax.broadcasted_iota(jnp.int32, (HD, 2 * HD), 1)).astype(bf16)
    zeros = jnp.zeros((HD, HD), f32)
    for h in range(HEADS):
        run[h] = eye2.astype(f32)

    def fold(c, carry):
        for h in range(HEADS):
            now = run[h]
            short = now.astype(bf16)
            pbs[c, h] = short
            run[h] = fin[c, h] * now - mm(ers[c, h], short) + jnp.concatenate([zeros, inj[c, h]], axis=1)
        return carry

    lax.fori_loop(0, TEN, fold, 0)
    for h in range(HEADS):
        pb[h] = run[h].astype(bf16)

    def unfold(c, carry):
        r = pl.ds(pl.multiple_of(c * CH, CH), CH)
        for h in range(HEADS):
            both = mm(rdr[c, h], pbs[c, h])
            rd[r, h * HD:(h + 1) * HD] = both[:, :HD].astype(bf16)
            lo[r, h * HD:(h + 1) * HD] = both[:, HD:] + loc[c, h]
        return carry

    def chain(later, earlier):
        p = mm(later[:, :HD], earlier)
        return (p + jnp.concatenate([zeros, later[:, HD:].astype(f32)], axis=1)).astype(bf16)

    chains = core == 0

    def up(h):
        return remote(pb.at[h], gc.at[me], upsem.at[0, h], upsem.at[1, me], column_dev(2 * h))

    def along(k):
        return remote(gx.at[cx], gx.at[cx], xsem.at[0, k], xsem.at[1, k], x_dev(k))

    def down(i):
        return remote(sb.at[i], sin.at[cy], downsem.at[0, i], downsem.at[1, cy], column_dev(i))

    def keeps(h):
        return chains & (cy == h)

    for h in range(HEADS):
        @pl.when(keeps(h))
        def _():
            gc[me] = pb[h]

        @pl.when(jnp.logical_not(keeps(h)))
        def _():
            up(h).start()

    other_half(1)
    many(2, 0, TEN)
    pairs(reads_of, 0, 4)

    @pl.when(chains)
    def _():
        for i in range(8):
            @pl.when(me != i)
            def _():
                remote(gc.at[i], gc.at[i], upsem.at[0, 0], upsem.at[1, i], column_dev(0)).wait_recv()
        two = [chain(gc[i + 1], gc[i]) for i in range(0, 8, 2)]
        four = [chain(two[1], two[0]), chain(two[3], two[2])]
        gx[cx] = chain(four[1], four[0])
        for k in (1, 2, 3):
            along(k).start()
        pre[0] = eye2
        pre[1] = gc[0]
        pre[2] = two[0]
        pre[3] = chain(gc[2], two[0])
        pre[4] = four[0]
        pre[5] = chain(gc[4], four[0])
        six = chain(two[2], four[0])
        pre[6] = six
        pre[7] = chain(gc[6], six)

    lax.fori_loop(0, TEN, unfold, 0)

    @pl.when(chains)
    def _():
        for k in (1, 2, 3):
            slot = gx.at[(cx + XN - k) % XN]
            remote(slot, slot, xsem.at[0, k], xsem.at[1, k], x_dev(k)).wait_recv()
        state = zeros
        begin[0] = state
        for k in range(XN - 1):
            state = mm(gx[k, :, :HD], state) + gx[k, :, HD:].astype(f32)
            begin[k + 1] = state
        state = begin[cx]
        for i in range(8):
            sb[i] = (mm(pre[i, :, :HD], state) + pre[i, :, HD:].astype(f32)).astype(bf16)

            @pl.when(me == i)
            def _():
                sin[cy] = sb[i]

            @pl.when(me != i)
            def _():
                down(i).start()

    for h in range(HEADS):
        @pl.when(jnp.logical_not(keeps(h)))
        def _():
            remote(sin.at[h], sin.at[h], downsem.at[0, 0], downsem.at[1, h], column_dev(0)).wait_recv()

    def attend(c):
        r = pl.ds(pl.multiple_of(c * CH, CH), CH)
        att = [mm(rd[r, h * HD:(h + 1) * HD], sin[h]) + lo[r, h * HD:(h + 1) * HD] for h in range(4)]
        for h in range(4):
            scale = lax.rsqrt(jnp.mean(att[h] * att[h], axis=-1, keepdims=True) + 1e-5)
            nrm[c, :, h * HD:(h + 1) * HD] = (att[h] * scale * gain[...]).astype(bf16)

    def partial(d, c):
        def tile(n, carry):
            at = pl.multiple_of(n * 384, 128)
            part[d, :, pl.ds(at, 384)] = mm_nt(nrm[c], wf[pl.ds(pl.multiple_of(d * HALF + at, 128), 384), OUT_AT:])
            return carry
        lax.fori_loop(0, HALF // 384, tile, 0)

    def send(d, t, u):
        rows = pl.ds(u * 64, 64)
        return remote(rsend.at[d, t, rows], rrecv.at[d, t, rows], rssem.at[d, t, u], rrsem.at[d, t, u], right if d == 0 else left)

    def ring(t, carry):
        def work(d, carry):
            c = (z + jnp.where(d == 0, 2 * TEN - 1 - t, 1 + t)) % TEN

            @pl.when((t < 3) | ((t == 3) & (d == 0)) | ((t == 7) & (d == 0)))
            def _():
                attend(c)

            partial(d, c)
            return carry

        lax.fori_loop(0, 2, work, 0)
        for u in range(2):
            rows = pl.ds(u * 64, 64)
            for d in range(2):
                @pl.when(t > 0)
                def _():
                    send(d, t - 1, u).wait_recv()
                    part[d, rows] += rrecv[d, t - 1, rows].astype(f32)

                @pl.when(t < 7)
                def _():
                    rsend[d, t, rows] = part[d, rows].astype(bf16)
                    send(d, t, u).start()
        return carry

    lax.fori_loop(0, 8, ring, 0)
    for d in range(2):
        out[:, d * HALF:(d + 1) * HALF] = part[d].astype(bf16)

    @pl.when(s < SEQ - 1)
    def _():
        for copy in rims:
            copy.wait_send()

    pair.wait_send()
    for copy in sends:
        copy().wait_send()
    for d in range(2):
        for k in range(1, 5):
            for i in range(2):
                if k < 4 or i == d:
                    x_copy(d, k, i).wait_send()
    for h in range(HEADS):
        @pl.when(jnp.logical_not(keeps(h)))
        def _():
            up(h).wait_send()

    @pl.when(chains)
    def _():
        for k in (1, 2, 3):
            along(k).wait_send()
        for i in range(8):
            @pl.when(me != i)
            def _():
                down(i).wait_send()


    def drain(t, carry):
        for d in range(2):
            for u in range(2):
                send(d, t, u).wait_send()
        return carry

    lax.fori_loop(0, 7, drain, 0)


def layer(x, w_qkv, w_beta, w_out, gate, taps, gain):
    vm, dma = pltpu.VMEM, pltpu.SemaphoreType.DMA
    whole = pl.BlockSpec(memory_space=pltpu.VMEM)
    return pl.pallas_call(
        layer_body,
        in_specs=[whole] * 4 + [pl.BlockSpec(memory_space=pl.ANY), whole, whole],
        out_specs=whole,
        out_shape=jax.ShapeDtypeStruct((CH, COLS), bf16),
        scratch_shapes=[
            vm((TEN, CH, COLS), bf16),
            vm((COLS, COLS), bf16),
            vm((PIECE, COLS), bf16),
            vm((PIECE, COLS), bf16),
            vm((PAIR, COLS), f32),
            vm((16, QKV), bf16),
            vm((TEN * CH + 16, QKV), bf16),
            vm((TEN * CH, 128), f32),
            vm((TEN * CH, WIDTH), f32),
            vm((TEN, HEADS, 1, HD), f32),
            vm((TEN, HEADS, CH, HD), bf16),
            vm((TEN, HEADS, CH, HD), bf16),
            vm((TEN, HEADS, CH, HD), bf16),
            vm((TEN, HEADS, CH, HD), bf16),
            vm((TEN, HEADS, CH, HD), bf16),
            vm((TEN, HEADS, CH, HD), bf16),
            vm((TEN, HEADS, CH, HD), f32),
            vm((TEN, HEADS, HD, HD), bf16),
            vm((TEN, HEADS, HD, HD), f32),
            vm((TEN, HEADS, HD, 1), f32),
            vm((TEN, HEADS, HD, 2 * HD), bf16),
            vm((HEADS, HD, 2 * HD), f32),
            vm((HEADS, HD, 2 * HD), bf16),
            vm((TEN * CH, WIDTH), bf16),
            vm((TEN * CH, WIDTH), f32),
            vm((8, HD, 2 * HD), bf16),
            vm((8, HD, 2 * HD), bf16),
            vm((XN, HD, 2 * HD), bf16),
            vm((XN, HD, HD), f32),
            vm((8, HD, HD), bf16),
            vm((HEADS, HD, HD), bf16),
            vm((TEN, CH, WIDTH), bf16),
            vm((2, CH, HALF), f32),
            vm((2, 7, CH, HALF), bf16),
            vm((2, 7, CH, HALF), bf16),
            dma((2, 4, 2)), dma((2, 4, 2)), dma((2, 16)), dma((2, 16)), dma((2, 16)), dma((2, 16)),
            dma((4,)), dma((4,)), dma((2,)), dma((2, 8)), dma((2, 4)), dma((2, 8)), dma((2, 7, 2)), dma((2, 7, 2)),
        ],
        compiler_params=pltpu.CompilerParams(collective_id=0, has_side_effects=True, vmem_limit_bytes=62 << 20),
    )(x, w_qkv, w_beta, w_out, gate, taps, gain)


def per_device(x_rows, w_qkv, w_beta, conv_weight, log_decay, norm_gain, w_out):
    return layer(x_rows, w_qkv.transpose(1, 0, 2), w_beta.T, w_out.T, log_decay, conv_weight.reshape(4, QKV), norm_gain.reshape(1, HD))


def solution(mesh):
    in_specs = (
        P(("seq", "tensor"), None),
        P("seq", None, "tensor"),
        P("seq", "tensor"),
        P(None, None, "tensor"),
        P("seq", "tensor"),
        P(),
        P("tensor", "seq"),
    )
    return jax.shard_map(per_device, mesh=mesh, in_specs=in_specs, out_specs=P(("seq", "tensor"), None), check_vma=False)
```

time: 155 us -> 140 us (0.903)
  Pallas kernels: 149 us -> 138 us
  local copies, waits for them, and re-layouts: 3.66 us -> 1.92 us
  other arithmetic: 1.64 us -> 0 us
    pallas_call x1, Pallas kernels: 149 us -> 138 us  [layer(): pl.pallas_call(layer_body, in_specs=[whole] * 4 + [pl.BlockSpec(memory_sp...]
    concatenate x1 -> x0, other arithmetic: 1.64 us -> none  [per_device(): jnp.concatenate([w_qkv.reshape(PIECE, BETA_AT), jnp.pad(w_beta, ((0, 0),...]
where the time goes in v3:
time: 140 us
  Pallas kernels  138 us (99%)
  local copies, waits for them, and re-layouts  1.92 us (1%)
    pallas_call x1, Pallas kernels, layer(): pl.pallas_call(layer_body, in_specs=[whole] * 4 + [pl.BlockSpec(memory_sp...  138 us

profile of v3, /device:TPU:1, one launch (start us, length us, event | category | flops | bytes accessed | tf_op | source)
XLA Modules:
  0.0 140.3 jit_solution(15685295994589855974)
XLA Ops:
  0.0 138.4 %shard_map.73 = bf16[128,2304]{1,0:T(8,128)(2,1)} custom-call(bf16[128,2304]{1,0:T(8,128)(2,1)} %x.1, bf16[3,72,512]{2,1,0:T(8,128)(2,1)} %bitcast.5, bf16[4,72]{1,0:T(4,128)(2,1)} %bitcast.8, bf16[72,512]{1,0:T(8,128)(2,1)} %bitcast.6, f32[1024,512]{1,0:T(8,128)} %gate_in.1, f32[4,1536]{1,0:T(4,128)} %bitcast.7, f32[1,128]{1,0:T(1,128)} %bitcast.9), custom_call_target="tpu_custom_call" | custom-call | tf_op jit(solution)/shard_map/pallas_call | solution.py:608
  138.4 1.9 %copy.10 = bf16[128,2304]{1,0:T(8,128)(2,1)} copy(bf16[128,2304]{1,0:T(8,128)(2,1)} %shard_map.73) | data formatting | bytes 1179648

commit v4 on v3

--- a/solution.py
+++ b/solution.py
@@ -185,10 +185,6 @@
         here = xg.at[(z + (TEN - k if d == 0 else k)) % TEN, pl.ds(64 * i, 64)]
         return remote(here, here, xs.at[d, k - 1, i], xr.at[d, k - 1, i], right if d == 0 else left)
 
-    for i in range(2):
-        for d in range(2):
-            x_copy(d, 1, i ^ d).start()
-
     w[:, :BETA_AT] = w_qkv[1]
     spread = (lax.broadcasted_iota(jnp.int32, (HEADS, V_AT - BETA_AT), 0) == lax.broadcasted_iota(jnp.int32, (HEADS, V_AT - BETA_AT), 1))
     w[:, BETA_AT:V_AT] = mm_tn(w_beta[...], spread).astype(bf16)
@@ -197,6 +193,10 @@
     w[:, OUT_AT:] = w_out[...]
     pair = remote(w, sib, ps.at[0], pr.at[0], other)
     pair.start()
+    for i in range(2):
+        for d in range(2):
+            x_copy(d, 1, i ^ d).start()
+
     own = pltpu.make_async_copy(x, xg.at[z], ls.at[0])
     own.start()
     decay = pltpu.make_async_copy(gate_in, gate, ls.at[1])
@@ -347,15 +347,14 @@
     side_blocks = [(2, 0), (3, 1), (1, 3), (3, 3), (1, 1)]
     far_blocks = [(2, 1), (2, 3), (0, 2), (3, 2), (1, 2), (2, 2)]
     first_hops(0)
+    relay_hops(0, near_blocks)
     x_forward(1, 0)
-    relay_hops(0, near_blocks)
     first_hops(1)
     x_forward(1, 1)
     relay_hops(0, side_blocks)
     relay_hops(1, near_blocks)
     x_forward(2, 0)
     relay_hops(0, far_blocks)
-    x_forward(2, 1)
     own.wait()
     decay.wait()
     other_half(0)
@@ -394,6 +393,7 @@
 
         @when(0)
         def _():
+            x_forward(2, 1)
             relay_hops(1, side_blocks)
 
         keys_of(t)
@@ -517,17 +517,19 @@
         def _():
             remote(sin.at[h], sin.at[h], downsem.at[0, 0], downsem.at[1, h], column_dev(0)).wait_recv()
 
-    def attend(c):
-        r = pl.ds(pl.multiple_of(c * CH, CH), CH)
-        att = [mm(rd[r, h * HD:(h + 1) * HD], sin[h]) + lo[r, h * HD:(h + 1) * HD] for h in range(4)]
-        for h in range(4):
-            scale = lax.rsqrt(jnp.mean(att[h] * att[h], axis=-1, keepdims=True) + 1e-5)
-            nrm[c, :, h * HD:(h + 1) * HD] = (att[h] * scale * gain[...]).astype(bf16)
-
-    def partial(d, c):
+    def attend(*chunks):
+        rows = [pl.ds(pl.multiple_of(c * CH, CH), CH) for c in chunks]
+        each = [(i, h) for i in range(len(chunks)) for h in range(HEADS)]
+        att = [mm(rd[rows[i], h * HD:(h + 1) * HD], sin[h]) + lo[rows[i], h * HD:(h + 1) * HD] for i, h in each]
+        for n, (i, h) in enumerate(each):
+            scale = lax.rsqrt(jnp.mean(att[n] * att[n], axis=-1, keepdims=True) + 1e-5)
+            nrm[chunks[i], :, h * HD:(h + 1) * HD] = (att[n] * scale * gain[...]).astype(bf16)
+
+    def partials(*chunks):
         def tile(n, carry):
             at = pl.multiple_of(n * 384, 128)
-            part[d, :, pl.ds(at, 384)] = mm_nt(nrm[c], wf[pl.ds(pl.multiple_of(d * HALF + at, 128), 384), OUT_AT:])
+            for d in range(2):
+                part[d, :, pl.ds(at, 384)] = mm_nt(nrm[chunks[d]], wf[pl.ds(pl.multiple_of(d * HALF + at, 128), 384), OUT_AT:])
             return carry
         lax.fori_loop(0, HALF // 384, tile, 0)
 
@@ -536,17 +538,17 @@
         return remote(rsend.at[d, t, rows], rrecv.at[d, t, rows], rssem.at[d, t, u], rrsem.at[d, t, u], right if d == 0 else left)
 
     def ring(t, carry):
-        def work(d, carry):
-            c = (z + jnp.where(d == 0, 2 * TEN - 1 - t, 1 + t)) % TEN
-
-            @pl.when((t < 3) | ((t == 3) & (d == 0)) | ((t == 7) & (d == 0)))
-            def _():
-                attend(c)
-
-            partial(d, c)
-            return carry
-
-        lax.fori_loop(0, 2, work, 0)
+        ahead, behind = (z + 2 * TEN - 1 - t) % TEN, (z + 1 + t) % TEN
+
+        @pl.when(t < 3)
+        def _():
+            attend(ahead, behind)
+
+        @pl.when((t == 3) | (t == 7))
+        def _():
+            attend(ahead)
+
+        partials(ahead, behind)
         for u in range(2):
             rows = pl.ds(u * 64, 64)
             for d in range(2):

time: 140 us -> 139 us (level)
  no operation moved by 1% of the time
where the time goes in v4:
time: 139 us
  Pallas kernels  137 us (99%)
  local copies, waits for them, and re-layouts  1.92 us (1%)
    pallas_call x1, Pallas kernels, layer(): pl.pallas_call(layer_body, in_specs=[whole] * 4 + [pl.BlockSpec(memory_sp...  137 us

profile of v4, /device:TPU:1, one launch (start us, length us, event | category | flops | bytes accessed | tf_op | source)
XLA Modules:
  0.0 139.1 jit_solution(17300300127742537992)
XLA Ops:
  0.0 137.2 %shard_map.73 = bf16[128,2304]{1,0:T(8,128)(2,1)} custom-call(bf16[128,2304]{1,0:T(8,128)(2,1)} %x.1, bf16[3,72,512]{2,1,0:T(8,128)(2,1)} %bitcast.5, bf16[4,72]{1,0:T(4,128)(2,1)} %bitcast.8, bf16[72,512]{1,0:T(8,128)(2,1)} %bitcast.6, f32[1024,512]{1,0:T(8,128)} %gate_in.1, f32[4,1536]{1,0:T(4,128)} %bitcast.7, f32[1,128]{1,0:T(1,128)} %bitcast.9), custom_call_target="tpu_custom_call" | custom-call | tf_op jit(solution)/shard_map/pallas_call | solution.py:610
  137.2 1.9 %copy.10 = bf16[128,2304]{1,0:T(8,128)(2,1)} copy(bf16[128,2304]{1,0:T(8,128)(2,1)} %shard_map.73) | data formatting | bytes 1179648

commit v5 on v4

--- a/solution.py
+++ b/solution.py
@@ -283,16 +283,19 @@
 
     def project(c, part):
         r = pl.multiple_of(16 + c * CH, 16)
-        at = (0, V_AT, Q_AT)[part]
-        acc = jnp.dot(xg[c], wf[:, at:at + WIDTH], preferred_element_type=f32)
-        proj[pl.ds(r, CH), part * WIDTH:(part + 1) * WIDTH] = acc.astype(bf16)
         if part == 0:
-            acc = jnp.dot(xg[c], wf[:, BETA_AT:BETA_AT + 128], preferred_element_type=f32)
-            logit[pl.ds(pl.multiple_of(c * CH, CH), CH)] = acc
+            acc = jnp.dot(xg[c], wf[:, :Q_AT], preferred_element_type=f32)
+            proj[pl.ds(r, CH), :WIDTH] = acc[:, :WIDTH].astype(bf16)
+            proj[pl.ds(r, CH), WIDTH:2 * WIDTH] = acc[:, V_AT:].astype(bf16)
+            logit[pl.ds(pl.multiple_of(c * CH, CH), CH)] = acc[:, BETA_AT:BETA_AT + 128]
+        else:
+            acc = jnp.dot(xg[c], wf[:, Q_AT:OUT_AT], preferred_element_type=f32)
+            proj[pl.ds(r, CH), 2 * WIDTH:] = acc.astype(bf16)
 
         @pl.when((c == TEN - 1) & (s < SEQ - 1))
         def _():
-            rims[part].start()
+            for n in ((0, 1) if part == 0 else (2,)):
+                rims[n].start()
 
     def pair_of(k):
         chunks = [(z + TEN - k) % TEN, (z + k + 1) % TEN]
@@ -389,7 +392,6 @@
         lo_n = jnp.where(t == 0, 0, 2 * t + 1)
         hi_n = jnp.minimum(2 * t + 3, TEN)
         many(0, lo_n, hi_n)
-        many(1, lo_n, hi_n)
 
         @when(0)
         def _():

time: 139 us -> 139 us (level)
  no operation moved by 1% of the time
where the time goes in v5:
time: 139 us
  Pallas kernels  137 us (99%)
  local copies, waits for them, and re-layouts  1.92 us (1%)
    pallas_call x1, Pallas kernels, layer(): pl.pallas_call(layer_body, in_specs=[whole] * 4 + [pl.BlockSpec(memory_sp...  137 us

profile of v5, /device:TPU:1, one launch (start us, length us, event | category | flops | bytes accessed | tf_op | source)
XLA Modules:
  0.0 138.5 jit_solution(7624773197037556426)
XLA Ops:
  0.0 136.6 %shard_map.73 = bf16[128,2304]{1,0:T(8,128)(2,1)} custom-call(bf16[128,2304]{1,0:T(8,128)(2,1)} %x.1, bf16[3,72,512]{2,1,0:T(8,128)(2,1)} %bitcast.5, bf16[4,72]{1,0:T(4,128)(2,1)} %bitcast.8, bf16[72,512]{1,0:T(8,128)(2,1)} %bitcast.6, f32[1024,512]{1,0:T(8,128)} %gate_in.1, f32[4,1536]{1,0:T(4,128)} %bitcast.7, f32[1,128]{1,0:T(1,128)} %bitcast.9), custom_call_target="tpu_custom_call" | custom-call | tf_op jit(solution)/shard_map/pallas_call | solution.py:612
  136.6 1.9 %copy.10 = bf16[128,2304]{1,0:T(8,128)(2,1)} copy(bf16[128,2304]{1,0:T(8,128)(2,1)} %shard_map.73) | data formatting | bytes 1179648
